TPU v7x, 256 devices: a whole 4x4x8 slice. The times are simulated.
256 devices in a mesh: row: 32 (over x, z), col: 8 (over y, core).
Axes of the slice: x: 4, y: 4, z: 8, core: 2. Of those that a mesh axis runs over, the one named last changes fastest.
Arguments:
- tokens: bfloat16 [4096, 5376], P('row', 'col'), may hold values from -6 to 6
- w_query: bfloat16 [5376, 4096], P('row', 'col'), may hold values from -0.078125 to 0.078125
- w_key: bfloat16 [5376, 2048], P('row', 'col'), may hold values from -0.078125 to 0.078125
- w_value: bfloat16 [5376, 2048], P('row', 'col'), may hold values from -0.078125 to 0.078125
- w_output: bfloat16 [4096, 5376], P('col', 'row'), may hold values from -0.09375 to 0.09375
- query_gain: float32 [128], replicated, may hold values from 0.1 to 1.9
- key_gain: float32 [128], replicated, may hold values from 0.1 to 1.9
- cotangent: bfloat16 [4096, 5376], P('row', 'col'), may hold values from -6 to 6
Outputs:
- layer_out: bfloat16 [4096, 5376], P('row', 'col')
- input_grad: bfloat16 [4096, 5376], P('row', 'col')
- grad_query: bfloat16 [5376, 4096], P('row', 'col')
- grad_key: bfloat16 [5376, 2048], P('row', 'col')
- grad_value: bfloat16 [5376, 2048], P('row', 'col')
- grad_output: bfloat16 [4096, 5376], P('col', 'row')
All inputs are finite; a program needn't handle non-finite values.
Results may differ from a plain program's by a relative error of at most 0.029.
Values may be sent and summed in bfloat16 or wider, within the bound.
A program may use at most 128 MiB of HBM per device.

v0:
```python
import jax
import jax.numpy as jnp
from jax import lax
from jax.sharding import PartitionSpec as P

WINDOW = 1024


query_scalar = 168.0
epsilon = 1e-06


def from_behind(value, axis, steps):
    count = lax.axis_size(axis)
    initial, last = (max(0, -steps), min(count, count - steps))
    return lax.ppermute(value, axis, [(source, source + steps) for source in range(initial, last)])


def rms_scale(values, gain_vector):
    mean_square = jnp.mean(values * values, axis=-1, keepdims=True)
    return values * lax.rsqrt(mean_square + epsilon) * gain_vector


def attend(queries, key_rows, value_rows, query_gain, key_gain, row_block, neighbours):
    length = queries.shape[0]
    head_width = query_gain.shape[0]
    groups = key_rows.shape[1] // head_width
    repeats = queries.shape[1] // (groups * head_width)
    key_total = key_rows.shape[0]
    query_heads = rms_scale(
        queries.reshape(length, groups, repeats, head_width), query_gain
    ) * query_scalar ** (-0.5)
    key_heads = rms_scale(key_rows.reshape(key_total, groups, head_width), key_gain)
    value_heads = value_rows.reshape(key_total, groups, head_width)
    scores = jnp.einsum("qgrd,kgd->grqk", query_heads, key_heads)
    query_index = row_block * length + jnp.arange(length, dtype=jnp.int32)
    key_index = (row_block - neighbours) * length + jnp.arange(key_total, dtype=jnp.int32)
    distance = query_index[:, None] - key_index[None, :]
    allowed = (distance >= 0) & (distance < WINDOW) & (key_index[None, :] >= 0)
    scores = jnp.where(allowed, scores, -1e30)
    row_max = lax.stop_gradient(jnp.max(scores, axis=-1, keepdims=True))
    exponent = jnp.exp(scores - row_max)
    weights = lax.optimization_barrier(
        (exponent / jnp.sum(exponent, axis=-1, keepdims=True)).astype(jnp.bfloat16)
    )
    blended = jnp.einsum("grqk,kgd->qgrd", weights.astype(jnp.float32), value_heads)
    return blended.reshape(length, groups * repeats * head_width)


def dot_last(left_side, right_side):
    return lax.dot_general(
        left_side, right_side, (((1,), (1,)), ((), ())), preferred_element_type=jnp.float32
    )


def dot_first(left_side, right_side):
    return lax.dot_general(
        left_side, right_side, (((0,), (0,)), ((), ())), preferred_element_type=jnp.float32
    )


def shards(tokens, w_query, w_key, w_value, w_output, query_gain, key_gain, cotangent):
    full_rows = lax.all_gather(tokens, "col", axis=1, tiled=True)
    row_count = full_rows.shape[0]
    neighbours = WINDOW // row_count
    row_block = lax.axis_index("row")
    query_cols = w_query.shape[1]
    key_cols = w_key.shape[1]
    full_output = lax.all_gather(w_output, "row", axis=1, tiled=True)
    pieces = (
        lax.all_gather(w_query, "row", axis=0, tiled=True),
        lax.all_gather(w_key, "row", axis=0, tiled=True),
        lax.all_gather(w_value, "row", axis=0, tiled=True),
    )
    columns = full_rows
    query_acc, key_acc, value_acc = tuple(
        (jnp.dot(columns, piece_part, preferred_element_type=jnp.float32) for piece_part in pieces)
    )
    queries = query_acc.astype(jnp.bfloat16)
    local_pair = jnp.concatenate(
        [key_acc.astype(jnp.bfloat16), value_acc.astype(jnp.bfloat16)], axis=1
    )
    pieces = [from_behind(local_pair, "row", distance) for distance in range(neighbours, 0, -1)]
    window_pairs = jnp.concatenate(pieces + [local_pair], axis=0).astype(jnp.float32)

    def attention_of(query_in, key_in, value_in):
        return attend(query_in, key_in, value_in, query_gain, key_gain, row_block, neighbours)

    blended, pullback = jax.vjp(
        attention_of,
        queries.astype(jnp.float32),
        window_pairs[:, :key_cols],
        window_pairs[:, key_cols:],
    )
    attended = blended.astype(jnp.bfloat16)
    layer_terms = jnp.dot(attended, full_output, preferred_element_type=jnp.float32)
    layer_out = lax.psum_scatter(
        layer_terms.astype(jnp.bfloat16), "col", scatter_dimension=1, tiled=True
    )
    grad_rows = lax.all_gather(cotangent, "col", axis=1, tiled=True)
    grad_attended = dot_last(grad_rows, full_output).astype(jnp.bfloat16)
    grad_queries, grad_keys, grad_values = pullback(grad_attended.astype(jnp.float32))
    pair_grads = jnp.concatenate([grad_keys, grad_values], axis=1)

    def block_rows(position):
        return pair_grads[position * row_count : (position + 1) * row_count]

    own_grads = block_rows(neighbours)
    for distance in range(1, neighbours + 1):
        own_grads = own_grads + from_behind(
            block_rows(neighbours - distance).astype(jnp.bfloat16), "row", -distance
        ).astype(jnp.float32)
    query_grad_bf = grad_queries.astype(jnp.bfloat16)
    key_grad_bf = own_grads[:, :key_cols].astype(jnp.bfloat16)
    value_grad_bf = own_grads[:, key_cols:].astype(jnp.bfloat16)
    pieces = lax.all_gather((w_query, w_key, w_value), "row", axis=0, tiled=True)
    input_terms = (
        dot_last(query_grad_bf, pieces[0])
        + dot_last(key_grad_bf, pieces[1])
        + dot_last(value_grad_bf, pieces[2])
    )
    input_grad = lax.psum_scatter(
        input_terms.astype(jnp.bfloat16), "col", scatter_dimension=1, tiled=True
    )
    stacked_grads = jnp.concatenate([query_grad_bf, key_grad_bf, value_grad_bf], axis=1)
    columns = full_rows
    projection_grads = lax.psum_scatter(
        dot_first(columns, stacked_grads).astype(jnp.bfloat16),
        "row",
        scatter_dimension=0,
        tiled=True,
    ).astype(jnp.float32)
    grad_query = projection_grads[:, :query_cols].astype(jnp.bfloat16)
    grad_key = projection_grads[:, query_cols : query_cols + key_cols].astype(jnp.bfloat16)
    grad_value = projection_grads[:, query_cols + key_cols :].astype(jnp.bfloat16)
    grad_output = lax.psum_scatter(
        dot_first(attended, grad_rows).astype(jnp.bfloat16), "row", scatter_dimension=1, tiled=True
    )
    return (layer_out, input_grad, grad_query, grad_key, grad_value, grad_output)


def solution(mesh):
    in_specs = (
        P("row", "col"),
        P("row", "col"),
        P("row", "col"),
        P("row", "col"),
        P("col", "row"),
        P(),
        P(),
        P("row", "col"),
    )
    out_specs = (
        P("row", "col"),
        P("row", "col"),
        P("row", "col"),
        P("row", "col"),
        P("row", "col"),
        P("col", "row"),
    )
    return jax.shard_map(shards, mesh=mesh, in_specs=in_specs, out_specs=out_specs, check_vma=False)
```

profile of v0, /device:TPU:1, one launch (start us, length us, event | category | flops | bytes accessed | tf_op | source)
XLA Modules:
  0.0 1036.6 jit_solution(6775664960634024463)
XLA Ops:
  11.2 1.5 fusion.30
  12.7 28.1 %all-gather.7.cloned.1.call-done = bf16[128,5376]{0,1:T(8,128)(2,1)} async-done(((bf16[128,672]{0,1:T(8,128)(2,1)}), bf16[128,5376]{0,1:T(8,128)(2,1)}) %all-gather.7.cloned.1.call-update) | async-done | bytes 1376272 | tf_op jit(solution)/shard_map/all_gather | solution.py:63
  40.8 77.9 %all-gather.11.cloned.1.call-done = bf16[5376,256]{1,0:T(8,128)(2,1)} async-done(((bf16[168,256]{1,0:T(8,128)(2,1)}), bf16[5376,256]{1,0:T(8,128)(2,1)}) %all-gather.11.cloned.1.call-update) | async-done | bytes 2752528 | tf_op jit(solution)/shard_map/all_gather | solution.py:73
  118.8 2.9 convolution_convert_fusion.7
  121.6 75.9 %all-gather.9.cloned.1.call-done = bf16[5376,256]{1,0:T(8,128)(2,1)} async-done(((bf16[168,256]{1,0:T(8,128)(2,1)}), bf16[5376,256]{1,0:T(8,128)(2,1)}) %all-gather.9.cloned.1.call-update) | async-done | bytes 2752528 | tf_op jit(solution)/shard_map/all_gather | solution.py:72
  197.6 2.4 convolution_convert_fusion.8
  200.0 2.0 collective-permute-start
  202.1 3.1 collective-permute-start.1
  205.7 3.0 collective-permute-start.2
  208.8 5.5 collective-permute-start.3
  214.2 4.3 collective-permute-start.4
  218.6 2.5 collective-permute-start.5
  221.1 4.0 collective-permute-start.6
  225.1 2.1 collective-permute-start.7
  227.3 3.4 collective-permute-done.5
  230.7 5.5 collective-permute-done.6
  236.2 6.7 collective-permute-done.7
  243.0 1.4 fusion.79
  244.4 1.9 reshape.107
  246.2 2.0 copy.81
  248.2 2.0 multiply_reduce_fusion.1
  250.4 1.8 reshape.98
  252.8 38.4 %all-gather.13.cloned.1.call-done = bf16[5376,512]{1,0:T(8,128)(2,1)} async-done(((bf16[168,512]{1,0:T(8,128)(2,1)}), bf16[5376,512]{1,0:T(8,128)(2,1)}) %all-gather.13.cloned.1.call-update) | async-done | bytes 5505040 | tf_op jit(solution)/shard_map/all_gather | solution.py:71
  291.2 3.5 fusion.24
  296.2 22.7 %all-gather.17.cloned.1.call-done = bf16[128,5376]{0,1:T(8,128)(2,1)} async-done(((bf16[128,672]{0,1:T(8,128)(2,1)}), bf16[128,5376]{0,1:T(8,128)(2,1)}) %all-gather.17.cloned.1.call-update) | async-done | bytes 1376272 | tf_op jit(solution)/shard_map/all_gather | solution.py:100
  318.9 86.2 %all-gather.15.cloned.1.call-done = bf16[512,5376]{0,1:T(8,128)(2,1)} async-done(((bf16[512,168]{0,1:T(8,128)(2,1)}), bf16[512,5376]{0,1:T(8,128)(2,1)}) %all-gather.15.cloned.1.call-update) | async-done | bytes 5505040 | tf_op jit(solution)/shard_map/all_gather | solution.py:69
  405.2 4.6 convolution_convert_fusion.4
  410.8 1.5 convolution_convert_fusion.3
  412.3 3.9 fusion.81
  416.9 2.5 fusion.14
  420.0 5.5 multiply_reduce_fusion
  425.6 5.1 multiply_reduce_fusion.2
  441.1 1.5 collective-permute-start.9
  445.6 2.3 collective-permute-done.11
  447.9 6.8 collective-permute-done.9
  454.7 9.2 collective-permute-done.8
  464.0 6.4 fusion.1
  470.4 14.7 %copy.118 = bf16[5376,1024]{1,0:T(8,128)(2,1)} copy(bf16[5376,1024]{0,1:T(8,128)(2,1)} %fusion.1) | data formatting | bytes 22020096
  485.5 5.2 convolution_convert_fusion.2
  490.8 4.3 fusion.89
  496.9 1.9 fusion.2
  500.2 4.0 convolution_convert_fusion.1
  504.2 221.7 %reduce-scatter.13.cloned.1.call-done = bf16[168,1024]{1,0:T(8,128)(2,1)} async-done(((bf16[5376,1024]{1,0:T(8,128)(2,1)}), bf16[168,1024]{1,0:T(8,128)(2,1)}) %reduce-scatter.13.cloned.1.call-update) | async-done | bytes 344080
  725.9 1.6 slice.93
  727.5 1.6 fusion.80
  729.1 35.0 %reduce-scatter.7.cloned.1.call-done = bf16[128,672]{0,1:T(8,128)(2,1)} async-done(((bf16[128,5376]{0,1:T(8,128)(2,1)}), bf16[128,672]{0,1:T(8,128)(2,1)}) %reduce-scatter.7.cloned.1.call-update) | async-done | bytes 172048 | tf_op jit(solution)/shard_map/reduce_scatter | solution.py:97
  764.1 36.9 %reduce-scatter.9.cloned.1.call-done = bf16[128,672]{0,1:T(8,128)(2,1)} async-done(((bf16[128,5376]{0,1:T(8,128)(2,1)}), bf16[128,672]{0,1:T(8,128)(2,1)}) %reduce-scatter.9.cloned.1.call-update) | async-done | bytes 172048 | tf_op jit(solution)/shard_map/reduce_scatter | solution.py:122
  801.0 228.8 %reduce-scatter.11.cloned.1.call-done = bf16[512,168]{0,1:T(8,128)(2,1)} async-done(((bf16[512,5376]{0,1:T(8,128)(2,1)}), bf16[512,168]{0,1:T(8,128)(2,1)}) %reduce-scatter.11.cloned.1.call-update) | async-done | bytes 172048 | tf_op jit(solution)/shard_map/reduce_scatter | solution.py:136
  (101 shorter events, 26.3 us)
Async XLA Ops:
  7.2 33.7 %all-gather.7.cloned.1.call-start = ((), (), s32[]{:S(2)}) async-start(), calls=%async_computation.4 | async-start | bytes 1548288 | tf_op jit(solution)/shard_map/all_gather | solution.py:63
  7.9 110.9 %all-gather.11.cloned.1.call-start = ((), (), s32[]{:S(2)}) async-start(), calls=%async_computation.6 | async-start | bytes 2838528 | tf_op jit(solution)/shard_map/all_gather | solution.py:73
  8.6 188.9 %all-gather.9.cloned.1.call-start = ((), (), s32[]{:S(2)}) async-start(), calls=%async_computation.5 | async-start | bytes 2838528 | tf_op jit(solution)/shard_map/all_gather | solution.py:72
  9.4 281.8 %all-gather.13.cloned.1.call-start = ((), (), s32[]{:S(2)}) async-start(), calls=%async_computation.7 | async-start | bytes 5677056 | tf_op jit(solution)/shard_map/all_gather | solution.py:71
  10.0 309.0 %all-gather.17.cloned.1.call-start = ((), (), s32[]{:S(2)}) async-start(), calls=%async_computation.10 | async-start | bytes 1548288 | tf_op jit(solution)/shard_map/all_gather | solution.py:100
  10.5 394.6 %all-gather.15.cloned.1.call-start = ((), (), s32[]{:S(2)}) async-start(), calls=%async_computation.8 | async-start | bytes 5677056 | tf_op jit(solution)/shard_map/all_gather | solution.py:69
  11.1 714.7 %reduce-scatter.13.cloned.1.call-start = ((), (), s32[]{:S(2)}) async-start(), calls=%async_computation.13 | async-start | bytes 11354112
  40.8 156.7 %copy-start.1 = (bf16[128,5376]{0,1:T(8,128)(2,1)S(1)}, bf16[128,5376]{0,1:T(8,128)(2,1)}, u32[]{:S(2)}) copy-start(bf16[128,5376]{0,1:T(8,128)(2,1)} %all-gather.7.cloned.1.call-done) | copy-start | bytes 4128772
  121.6 83.5 %copy-start.14 = (f32[128]{0:T(128)S(1)}, f32[128]{0:T(128)}, u32[]{:S(2)}) copy-start(f32[128]{0:T(128)} %param.13) | copy-start | bytes 1540
  200.0 18.5 %collective-permute-start = (bf16[128,512]{1,0:T(8,128)(2,1)S(1)}, bf16[128,512]{1,0:T(8,128)(2,1)S(1)}, u32[]{:S(2)}, u32[]{:S(2)}) collective-permute-start(bf16[128,512]{1,0:T(8,128)(2,1)S(1)} %pad_maximum_fusion.1), channel_id=1, source_target_pairs={{0,64},{8,72},{16,80},{24,88},{32,96},{40,104},{48,112},{56,120},{... | collective-permute-start | bytes 393224 | tf_op jit(solution)/shard_map/ppermute | solution.py:16
  202.1 19.0 %collective-permute-start.1 = (bf16[128,512]{1,0:T(8,128)(2,1)S(1)}, bf16[128,512]{1,0:T(8,128)(2,1)S(1)}, u32[]{:S(2)}, u32[]{:S(2)}) collective-permute-start(bf16[128,512]{1,0:T(8,128)(2,1)S(1)} %pad_maximum_fusion.1), channel_id=1, source_target_pairs={{0,56},{8,64},{16,72},{24,80},{32,88},{40,96},{48,104},{56,112},{6... | collective-permute-start | bytes 393224 | tf_op jit(solution)/shard_map/ppermute | solution.py:16
  205.7 19.4 %collective-permute-start.2 = (bf16[128,512]{1,0:T(8,128)(2,1)S(1)}, bf16[128,512]{1,0:T(8,128)(2,1)S(1)}, u32[]{:S(2)}, u32[]{:S(2)}) collective-permute-start(bf16[128,512]{1,0:T(8,128)(2,1)S(1)} %pad_maximum_fusion.1), channel_id=1, source_target_pairs={{0,48},{8,56},{16,64},{24,72},{32,80},{40,88},{48,96},{56,104},{64... | collective-permute-start | bytes 393224 | tf_op jit(solution)/shard_map/ppermute | solution.py:16
  208.8 18.5 %collective-permute-start.3 = (bf16[128,512]{1,0:T(8,128)(2,1)S(1)}, bf16[128,512]{1,0:T(8,128)(2,1)S(1)}, u32[]{:S(2)}, u32[]{:S(2)}) collective-permute-start(bf16[128,512]{1,0:T(8,128)(2,1)S(1)} %pad_maximum_fusion.1), channel_id=1, source_target_pairs={{0,40},{8,48},{16,56},{24,64},{32,72},{40,80},{48,88},{56,96},{64,... | collective-permute-start | bytes 393224 | tf_op jit(solution)/shard_map/ppermute | solution.py:16
  214.2 13.0 %collective-permute-start.4 = (bf16[128,512]{1,0:T(8,128)(2,1)S(1)}, bf16[128,512]{1,0:T(8,128)(2,1)S(1)}, u32[]{:S(2)}, u32[]{:S(2)}) collective-permute-start(bf16[128,512]{1,0:T(8,128)(2,1)S(1)} %pad_maximum_fusion.1), channel_id=1, source_target_pairs={{0,32},{8,40},{16,48},{24,56},{32,64},{40,72},{48,80},{56,88},{64,... | collective-permute-start | bytes 393224 | tf_op jit(solution)/shard_map/ppermute | solution.py:16
  218.6 12.1 %collective-permute-start.5 = (bf16[128,512]{1,0:T(8,128)(2,1)S(1)}, bf16[128,512]{1,0:T(8,128)(2,1)S(1)}, u32[]{:S(2)}, u32[]{:S(2)}) collective-permute-start(bf16[128,512]{1,0:T(8,128)(2,1)S(1)} %pad_maximum_fusion.1), channel_id=1, source_target_pairs={{0,24},{8,32},{16,40},{24,48},{32,56},{40,64},{48,72},{56,80},{64,... | collective-permute-start | bytes 393224 | tf_op jit(solution)/shard_map/ppermute | solution.py:16
  221.1 15.1 %collective-permute-start.6 = (bf16[128,512]{1,0:T(8,128)(2,1)S(1)}, bf16[128,512]{1,0:T(8,128)(2,1)S(1)}, u32[]{:S(2)}, u32[]{:S(2)}) collective-permute-start(bf16[128,512]{1,0:T(8,128)(2,1)S(1)} %pad_maximum_fusion.1), channel_id=1, source_target_pairs={{0,16},{8,24},{16,32},{24,40},{32,48},{40,56},{48,64},{56,72},{64,... | collective-permute-start | bytes 393224 | tf_op jit(solution)/shard_map/ppermute | solution.py:16
  225.1 17.8 %collective-permute-start.7 = (bf16[128,512]{1,0:T(8,128)(2,1)S(1)}, bf16[128,512]{1,0:T(8,128)(2,1)S(1)}, u32[]{:S(2)}, u32[]{:S(2)}) collective-permute-start(bf16[128,512]{1,0:T(8,128)(2,1)S(1)} %pad_maximum_fusion.1), channel_id=1, source_target_pairs={{0,8},{8,16},{16,24},{24,32},{32,40},{40,48},{48,56},{56,64},{64,7... | collective-permute-start | bytes 393224 | tf_op jit(solution)/shard_map/ppermute | solution.py:16
  295.0 130.5 %copy-start.7 = (f32[128,2,2,128]{0,3,2,1:T(8,128)}, f32[128,2,2,128]{0,3,2,1:T(8,128)S(1)}, u32[]{:S(2)}) copy-start(f32[128,2,2,128]{0,3,2,1:T(8,128)S(1)} %copy.83) | copy-start | bytes 786436
  409.7 2.6 copy-start.4
  430.7 0.7 copy-start.11
  430.7 1.3 copy-start.5
  430.7 1.6 copy-start.6
  430.7 1.6 copy-start.10
  432.7 6.8 copy-start.13
  432.7 12.1 %copy-start.8 = (f32[128,2,2,128]{0,3,2,1:T(8,128)S(1)}, f32[128,2,2,128]{0,3,2,1:T(8,128)}, u32[]{:S(2)}) copy-start(f32[128,2,2,128]{0,3,2,1:T(8,128)} %copy-done.7) | copy-start | bytes 786436
  432.7 12.1 %copy-start.9 = (f32[128,2,2,128]{0,3,2,1:T(8,128)S(1)}, f32[128,2,2,128]{0,3,2,1:T(8,128)}, u32[]{:S(2)}) copy-start(f32[128,2,2,128]{0,3,2,1:T(8,128)} %get-tuple-element.47) | copy-start | bytes 786436
  432.7 12.1 %copy-start.12 = (f32[128,2,2]{0,2,1:T(2,128)S(1)}, f32[128,2,2]{0,2,1:T(2,128)}, u32[]{:S(2)}) copy-start(f32[128,2,2]{0,2,1:T(2,128)} %fusion.58) | copy-start | bytes 6148
  432.9 6.5 collective-permute-start.15
  434.2 6.9 collective-permute-start.14
  435.5 7.9 collective-permute-start.13
  436.8 8.8 collective-permute-start.12
  438.1 9.8 collective-permute-start.11
  439.4 8.5 collective-permute-start.10
  441.1 13.5 %collective-permute-start.9 = (bf16[128,512]{0,1:T(8,128)(2,1)S(1)}, bf16[128,512]{0,1:T(8,128)(2,1)S(1)}, u32[]{:S(2)}, u32[]{:S(2)}) collective-permute-start(bf16[128,512]{0,1:T(8,128)(2,1)S(1)} %get-tuple-element.39), channel_id=1, source_target_pairs={{16,0},{24,8},{32,16},{40,24},{48,32},{56,40},{64,48},{72,56},{80,... | collective-permute-start | bytes 393224 | tf_op jit(solution)/shard_map/ppermute | solution.py:16
  443.4 20.4 %collective-permute-start.8 = (bf16[128,512]{0,1:T(8,128)(2,1)S(1)}, bf16[128,512]{0,1:T(8,128)(2,1)S(1)}, u32[]{:S(2)}, u32[]{:S(2)}) collective-permute-start(bf16[128,512]{0,1:T(8,128)(2,1)S(1)} %get-tuple-element.32), channel_id=1, source_target_pairs={{8,0},{16,8},{24,16},{32,24},{40,32},{48,40},{56,48},{64,56},{72,6... | collective-permute-start | bytes 393224 | tf_op jit(solution)/shard_map/ppermute | solution.py:16
  485.1 279.0 %reduce-scatter.7.cloned.1.call-start = ((), (), s32[]{:S(2)}) async-start(), calls=%async_computation.9 | async-start | bytes 1548288 | tf_op jit(solution)/shard_map/reduce_scatter | solution.py:97
  490.8 310.2 %reduce-scatter.9.cloned.1.call-start = ((), (), s32[]{:S(2)}) async-start(), calls=%async_computation.11 | async-start | bytes 1548288 | tf_op jit(solution)/shard_map/reduce_scatter | solution.py:122
  490.8 4.3 copy-start.2
  495.2 1.8 copy-start
  498.9 1.3 copy-start.3
  498.9 530.9 %reduce-scatter.11.cloned.1.call-start = ((), (), s32[]{:S(2)}) async-start(), calls=%async_computation.12 | async-start | bytes 5677056 | tf_op jit(solution)/shard_map/reduce_scatter | solution.py:136
Sparse Core Ops, SparseCore 0:
  9.8 30.9 all-gather.6
  43.4 75.2 all-gather.10
  121.4 76.1 all-gather.8
  200.0 91.1 all-gather.12
  292.9 26.0 all-gather.16
  321.4 83.7 all-gather.14
  485.2 240.6 reduce-scatter.12
  729.1 34.9 reduce-scatter.6
  767.2 33.7 reduce-scatter.8
  805.9 223.8 reduce-scatter.10
where the time goes:
time: 1040 us
  waiting for transfers between devices  891 us (86%)
  matrix products  53 us (5%)
  starting transfers between devices  37.4 us (4%)
  local copies, waits for them, and re-layouts  28.9 us (3%)
  between operations  14.7 us (1%)
  other arithmetic  11.4 us (1%)
    reduce_scatter x1, waiting for transfers between devices, shards(): lax.psum_scatter(dot_first(attended, grad_rows).astype(jnp.bfloat16), 'ro...  229 us
    unnamed x11, waiting for transfers between devices  225 us
    all_gather x1, waiting for transfers between devices, shards(): full_output = lax.all_gather(w_output, 'row', axis=1, tiled=True)  86.2 us
    all_gather x1, waiting for transfers between devices, shards(): lax.all_gather(w_value, 'row', axis=0, tiled=True)  77.9 us
    all_gather x1, waiting for transfers between devices, shards(): lax.all_gather(w_key, 'row', axis=0, tiled=True)  75.9 us
    all_gather x1, waiting for transfers between devices, shards(): lax.all_gather(w_query, 'row', axis=0, tiled=True)  38.4 us
    ppermute x16, starting transfers between devices, from_behind(): lax.ppermute(value, axis, [(source, source + steps) for source in range(i...  37 us
    reduce_scatter x1, waiting for transfers between devices, shards(): lax.psum_scatter(input_terms.astype(jnp.bfloat16), 'col', scatter_dimensi...  36.9 us
  transfers between devices with their start and end apart: 26, of which 19 were waited for; matrix products, arithmetic and copies ran while one was open for 4% of the time, Pallas kernels for 0%

commit v1 on v0

v1 whole, which is shorter than its diff:
```python
import functools

import jax
import jax.numpy as jnp
from jax import lax
from jax.experimental import pallas as pl
from jax.experimental.pallas import tpu as pltpu
from jax.sharding import PartitionSpec as P

BF16 = jnp.bfloat16
F32 = jnp.float32

NX, NZ, NY = 4, 8, 4

OWN, SENT, PITCH, BLOCK = 168, 176, 192, 768
TOK = 128
SLAB = 2 * TOK
HD = 128
BACK = 4
KEYS = (BACK + 1) * SLAB
WINDOW = 1024
QKV, OUT = 0, 1
WIDTH = (512, 256)
query_scalar = 168.0
epsilon = 1e-06


def dot(a, b, ca, cb):
    return lax.dot_general(a, b, (((ca,), (cb,)), ((), ())), preferred_element_type=F32)


def remainder(a, b):
    return lax.rem(a + b, b)


def near_first(i):
    odd = lax.rem(i, 2)
    return odd * lax.div(i + 1, 2) + (1 - odd) * lax.rem(8 - lax.div(i, 2), 8)


def spread():
    i = lax.broadcasted_iota(jnp.int32, (4 * OWN, BLOCK), 0)
    j = lax.broadcasted_iota(jnp.int32, (4 * OWN, BLOCK), 1)
    group = (
        (i >= OWN).astype(jnp.int32)
        + (i >= 2 * OWN).astype(jnp.int32)
        + (i >= 3 * OWN).astype(jnp.int32)
    )
    return (j == i + (PITCH - OWN) * group).astype(F32).astype(BF16)


def kernel(
    tok_in, cot_in, wq_in, wk_in, wv_in, wo_in, qg_ref, kg_ref,
    layer_out, input_grad, gq_out, gk_out, gv_out, go_out,
    place, tok, cot, pack_qkv, pack_out, w_qkv, w_out, g_qkv, g_out,
    acc, q_raw, qh, kh, kvwin, scores, pb, ds, att, datt, dkv, dkv_own, dkv_in, dqkv,
    ybuf, ysib, yrecv, zbuf, zsib, zrecv,
    relay_qkv, relay_out, full_qkv, full_out, ring_qkv, ring_out,
    s_loc, s_z, r_z, s_xf, r_xf, s_xh, r_xh, s_t, r_t, s_s, r_s, s_kv, r_kv, s_dk, r_dk,
    s_rl, r_rl, s_fl, r_fl, s_rz, r_rz, s_ys, r_ys, s_yy, r_yy,
):
    row = lax.axis_index("row")
    col = lax.axis_index("col")
    x, z = lax.div(row, NZ), lax.rem(row, NZ)
    y, core = lax.div(col, 2), lax.rem(col, 2)
    par = lax.rem(z, 2)
    pair = lax.div(row, 2)
    xs = [x, lax.rem(x + 1, NX), lax.rem(x + 2, NX), lax.rem(x + 3, NX)]
    sibling = col + 1 - 2 * core

    def remote(src, dst, ssem, rsem, to_row, to_col):
        return pltpu.make_async_remote_copy(
            src_ref=src, dst_ref=dst, send_sem=ssem, recv_sem=rsem,
            device_id={"row": to_row, "col": to_col}, device_id_type=pl.DeviceIdType.MESH,
        )

    def ring_row(d):
        return x * NZ + lax.rem(z + d, NZ)

    def group_at(e, sign):
        dy, dq = lax.div(e, 2), lax.rem(e, 2)
        yt = lax.rem(y + NY + sign * dy, NY)
        return row + dq * (1 - 2 * par), yt * 2 + core

    def back_row(i):
        return 2 * lax.rem(pair + 16 - i, 16) + par

    barrier = pltpu.get_barrier_semaphore()

    def greet(to_row, to_col):
        pl.semaphore_signal(
            barrier, inc=1, device_id={"row": to_row, "col": to_col},
            device_id_type=pl.DeviceIdType.MESH,
        )

    @pl.loop(1, 8)
    def _(d):
        greet(ring_row(d), col)
        gr, gc = group_at(d, 1)
        greet(gr, gc)

    @pl.loop(1, BACK + 1)
    def _(i):
        greet(back_row(i), col)
        greet(back_row(16 - i), col)

    greet(row, sibling)
    greet(xs[1] * NZ + z, col)
    greet(xs[3] * NZ + z, col)

    packs = (pack_qkv, pack_out)
    fulls_w = (w_qkv, w_out)
    grads = (g_qkv, g_out)

    def rows_of(xx, zz):
        return 2 * xx + lax.div(zz, 4), pl.ds(pl.multiple_of(PITCH * lax.rem(zz, 4), 16), SENT)

    def block(ref, xx, zz):
        c, rows = rows_of(xx, zz)
        return ref.at[c, rows]

    def half_of(a, side):
        return pl.ds(side * (WIDTH[a] // 2), WIDTH[a] // 2)

    def half(ref, a, xx, zz, side):
        c, rows = rows_of(xx, zz)
        return ref.at[c, rows, half_of(a, side)]

    for q in (0, 1):
        pack_qkv[q, 160:SENT, :] = jnp.zeros((16, 512), BF16)
        pack_qkv[q, 0:OWN, 0:256] = wq_in[:, 256 * q : 256 * q + 256]
        pack_qkv[q, 0:OWN, 256:384] = wk_in[:, 128 * q : 128 * q + 128]
        pack_qkv[q, 0:OWN, 384:512] = wv_in[:, 128 * q : 128 * q + 128]
        pack_out[q, 160:SENT, :] = jnp.zeros((16, 256), BF16)
        pack_out[q, 0:OWN, :] = wo_in[:, 256 * q : 256 * q + 256]

    pl.semaphore_wait(barrier, 25)

    def z_copy(a, d, zs, zt):
        return remote(
            packs[a].at[lax.rem(zt, 2)], block(fulls_w[a], x, zs),
            s_z.at[a, d], r_z.at[a, d], x * NZ + zt, col,
        )

    def z_start(a):
        pltpu.make_async_copy(packs[a].at[par], block(fulls_w[a], x, z), s_loc.at[a]).start()

        @pl.loop(1, 8)
        def _(i):
            d = near_first(i)
            z_copy(a, d, z, lax.rem(z + d, NZ)).start()

    z_start(QKV)

    place[...] = spread()
    own_rows = pl.ds(pl.multiple_of(TOK * par, TOK), TOK)

    def t_slot(ref, e, cc):
        dy, dq = lax.div(e, 2), lax.rem(e, 2)
        c = lax.rem(y + NY - dy, NY) * 2 + cc
        q = par + dq * (1 - 2 * par)
        return ref.at[c, pl.ds(pl.multiple_of(TOK * q, TOK), TOK)]

    slabs = (tok, cot)

    def t_copy(t, e):
        gr, gc = group_at(e, 1)
        own = slabs[t].at[col, own_rows]
        return remote(own, own, s_t.at[t, e], r_t.at[t, e], gr, gc)

    def t_recv(t, e):
        gr, gc = group_at(e, 1)
        slot = t_slot(slabs[t], e, core)
        return remote(slot, slot, s_t.at[t, e], r_t.at[t, e], gr, gc)

    def sib_copy(t, e, cc):
        slot = t_slot(slabs[t], e, cc)
        return remote(slot, slot, s_s.at[t, e], r_s.at[t, e], row, sibling)

    for t, src in ((0, tok_in), (1, cot_in)):
        slabs[t][col, own_rows] = dot(src[...], place[...], 1, 0).astype(BF16)

        @pl.loop(1, 8)
        def _(e):
            t_copy(t, e).start()

        sib_copy(t, 0, core).start()

    for c in range(8):
        for j in range(4):
            gap = slice(PITCH * j + SENT, PITCH * (j + 1))
            w_qkv[c, gap, :] = jnp.zeros((PITCH - SENT, 512), BF16)
            w_out[c, gap, :] = jnp.zeros((PITCH - SENT, 256), BF16)

    def xf_copy(a, i, side, xx):
        slot = block(fulls_w[a], xx, remainder(z - near_first(i), NZ))
        to = xs[1] if side == 0 else xs[3]
        return remote(slot, slot, s_xf.at[a, side, i], r_xf.at[a, side, i], to * NZ + z, col)

    def xh_copy(a, i, side, xx):
        slot = half(fulls_w[a], a, xx, remainder(z - near_first(i), NZ), side)
        to = xs[1] if side == 0 else xs[3]
        return remote(slot, slot, s_xh.at[a, side, i], r_xh.at[a, side, i], to * NZ + z, col)

    def gather_first(a, i, own):
        if own:
            pltpu.make_async_copy(packs[a].at[par], block(fulls_w[a], x, z), s_loc.at[a]).wait()
        else:
            d = near_first(i)
            z_copy(a, d, remainder(z - d, NZ), z).wait_recv()
        xf_copy(a, i, 0, x).start()
        xf_copy(a, i, 1, x).start()

    def gather_second(a, i):
        xf_copy(a, i, 0, xs[3]).wait_recv()
        xh_copy(a, i, 0, xs[3]).start()
        xf_copy(a, i, 1, xs[1]).wait_recv()
        xh_copy(a, i, 1, xs[1]).start()

    def gather_third(a, i):
        xh_copy(a, i, 0, xs[2]).wait_recv()
        xh_copy(a, i, 1, xs[2]).wait_recv()

    def share(t):
        @pl.loop(1, 8)
        def _(e):
            t_recv(t, e).wait_recv()
            sib_copy(t, e, core).start()

    def shared(t):
        @pl.loop(0, 8)
        def _(e):
            sib_copy(t, e, 1 - core).wait_recv()

    zero = jnp.int32(0)
    gather_first(QKV, zero, True)

    @pl.loop(1, 8)
    def _(i):
        gather_first(QKV, i, False)
        gather_second(QKV, i - 1)

    z_start(OUT)
    gather_second(QKV, jnp.int32(7))
    share(0)
    shared(0)

    acc[...] = jnp.zeros_like(acc)

    def project(xx):
        @pl.loop(0, 2)
        def _(cc):
            c = 2 * xx + cc
            acc[...] += dot(tok[c], w_qkv[c], 1, 0)

    project(xs[0])
    project(xs[1])
    project(xs[3])

    gather_first(OUT, zero, True)

    @pl.loop(1, 8)
    def _(i):
        gather_first(OUT, i, False)

    @pl.loop(0, 8)
    def _(i):
        gather_third(QKV, i)

    project(xs[2])

    own_keys = pl.ds(BACK * SLAB, SLAB)
    kvwin[own_keys, :] = acc[:, 256:512].astype(BF16)

    def kv_copy(i):
        return remote(
            kvwin.at[own_keys], kvwin.at[pl.ds((BACK - i) * SLAB, SLAB)],
            s_kv.at[i - 1], r_kv.at[i - 1], back_row(16 - i), col,
        )

    for i in range(1, BACK + 1):
        kv_copy(i).start()

    def scale_of(values):
        return lax.rsqrt(jnp.mean(values * values, axis=-1, keepdims=True) + epsilon)

    qgain = qg_ref[...] * query_scalar ** (-0.5)
    kgain = kg_ref[...]
    for h in range(2):
        lanes = slice(HD * h, HD * h + HD)
        q = acc[:, lanes].astype(BF16)
        q_raw[:, lanes] = q
        q = q.astype(F32)
        qh[SLAB * h : SLAB * h + SLAB, :] = (q * scale_of(q) * qgain).astype(BF16)

    share(1)

    @pl.loop(0, 8)
    def _(i):
        gather_second(OUT, i)

    for i in range(1, BACK + 1):
        kv_copy(i).wait_recv()

    @pl.loop(0, BACK + 1)
    def _(s):
        rows = pl.ds(pl.multiple_of(s * SLAB, SLAB), SLAB)
        k = kvwin[rows, 0:HD].astype(F32)
        kh[rows, :] = (k * scale_of(k) * kgain).astype(BF16)

    scores[...] = dot(qh[...], kh[...], 1, 1)
    chunk = 32
    first_key = WINDOW - SLAB * pair

    @pl.loop(0, 2 * SLAB // chunk)
    def _(n):
        rows = pl.ds(pl.multiple_of(n * chunk, chunk), chunk)
        t0 = lax.rem(n, SLAB // chunk) * chunk
        t = t0 + lax.broadcasted_iota(jnp.int32, (chunk, 1), 0)
        key = lax.broadcasted_iota(jnp.int32, (chunk, KEYS), 1)
        allowed = (key <= t + WINDOW) & (key >= jnp.maximum(t + 1, first_key))
        s = jnp.where(allowed, scores[rows, :], -1e30)
        e = jnp.exp(s - jnp.max(s, axis=-1, keepdims=True))
        pb[rows, :] = (e * (1.0 / jnp.sum(e, axis=-1, keepdims=True))).astype(BF16)

    blended = dot(pb[...], kvwin[:, HD:], 1, 0).astype(BF16)
    att[:, 0:HD] = blended[0:SLAB]
    att[:, HD:] = blended[SLAB:]

    shared(1)

    relays = (relay_qkv, relay_out)
    fulls = (full_qkv, full_out)
    rings = (ring_qkv, ring_out)

    def rl_copy(a, zz, side):
        to = xs[1] if side == 0 else xs[3]
        return remote(
            half(grads[a], a, xs[2], zz, side), relays[a].at[side, zz],
            s_rl.at[a, side, zz], r_rl.at[a, side, zz], to * NZ + z, col,
        )

    def fl_copy(a, zz, side):
        to = xs[1] if side == 0 else xs[3]
        return remote(
            block(grads[a], to, zz), fulls[a].at[side, zz],
            s_fl.at[a, side, zz], r_fl.at[a, side, zz], to * NZ + z, col,
        )

    def rz_copy(a, d, slot):
        zt = lax.rem(z + d, NZ)
        return remote(
            block(grads[a], x, zt), rings[a].at[slot],
            s_rz.at[a, d], r_rz.at[a, d], x * NZ + zt, col,
        )

    def far_first(i):
        return lax.rem(z + near_first(7 - i), NZ)

    def reduce_start(a):
        @pl.loop(0, 8)
        def _(i):
            rl_copy(a, far_first(i), 0).start()
            rl_copy(a, far_first(i), 1).start()

    def reduce_second(a, i):
        zz = far_first(i)
        for side in (0, 1):
            rl_copy(a, zz, side).wait_recv()
            to = xs[1] if side == 0 else xs[3]
            c, rows = rows_of(to, zz)
            lanes = half_of(a, side)
            grads[a][c, rows, lanes] = (
                grads[a][c, rows, lanes].astype(F32) + relays[a][side, zz].astype(F32)
            ).astype(BF16)
            fl_copy(a, zz, side).start()

    def reduce_third(a, i, own):
        zz = far_first(i)
        fl_copy(a, zz, 0).wait_recv()
        fl_copy(a, zz, 1).wait_recv()
        c, rows = rows_of(x, zz)
        total = (
            grads[a][c, rows, :].astype(F32)
            + fulls[a][0, zz].astype(F32)
            + fulls[a][1, zz].astype(F32)
        ).astype(BF16)
        if own:
            rings[a][z] = total
        else:
            grads[a][c, rows, :] = total
            rz_copy(a, near_first(7 - i), z).start()

    def reduce_last(a, q):
        total = rings[a][q].astype(F32)
        for k in (2, 4, 6):
            total = total + rings[a][q + k].astype(F32)
        return total.astype(BF16)

    def reduce_middle(a):
        reduce_second(a, zero)

        @pl.loop(1, 8)
        def _(i):
            reduce_second(a, i)
            reduce_third(a, i - 1, False)

        reduce_third(a, jnp.int32(7), True)

    def reduce_wait(a):
        @pl.loop(1, 8)
        def _(d):
            rz_copy(a, d, remainder(z - d, NZ)).wait_recv()

    ybufs, ysibs, yrecvs = (ybuf, zbuf), (ysib, zsib), (yrecv, zrecv)

    def ys_copy(t, yy):
        return remote(
            ybufs[t].at[2 * yy + 1 - core], ysibs[t].at[yy],
            s_ys.at[t, yy], r_ys.at[t, yy], row, sibling,
        )

    def yy_copy(t, e):
        gr, gc = group_at(e, 1)
        q = par + lax.rem(e, 2) * (1 - 2 * par)
        return remote(
            ybufs[t].at[gc, pl.ds(pl.multiple_of(TOK * q, TOK), TOK)], yrecvs[t].at[e],
            s_yy.at[t, e], r_yy.at[t, e], gr, gc,
        )

    def sum_start(t):
        @pl.loop(0, NY)
        def _(yy):
            ys_copy(t, yy).start()

    def sum_second(t):
        @pl.loop(0, NY)
        def _(i):
            dy = lax.rem(i + 2, NY)
            yy = lax.rem(y + dy, NY)
            ys_copy(t, yy).wait_recv()
            c = 2 * yy + core
            ybufs[t][c] = (ybufs[t][c].astype(F32) + ysibs[t][yy].astype(F32)).astype(BF16)

            @pl.when(i != 2)
            def _():
                yy_copy(t, 2 * dy).start()

            yy_copy(t, 2 * dy + 1).start()

    def sum_last(t, out):
        @pl.loop(1, 8)
        def _(e):
            yy_copy(t, e).wait_recv()

        total = ybufs[t][col, own_rows].astype(F32)
        for e in range(1, 8):
            total = total + yrecvs[t][e].astype(F32)
        out[...] = dot(total.astype(BF16), place[...], 1, 1).astype(BF16)

    for k in (2, 1, 3, 0):
        @pl.loop(0, 2)
        def _(cc):
            c = 2 * xs[k] + cc
            g_out[c] = dot(cot[c], att[...], 0, 0).astype(BF16)

        if k == 2:
            reduce_start(OUT)

    @pl.loop(0, 8)
    def _(i):
        gather_third(OUT, i)

    acc[:, 0:256] = jnp.zeros((SLAB, 256), F32)

    @pl.loop(0, 8)
    def _(c):
        acc[:, 0:256] += dot(cot[c], w_out[c], 1, 0)
        ybuf[c] = dot(att[...], w_out[c], 1, 1).astype(BF16)

    sum_start(0)
    for h in range(2):
        datt[SLAB * h : SLAB * h + SLAB, :] = acc[:, HD * h : HD * h + HD].astype(BF16)

    scores[...] = dot(datt[...], kvwin[:, HD:], 1, 1)

    @pl.loop(0, 2 * SLAB // chunk)
    def _(n):
        rows = pl.ds(pl.multiple_of(n * chunk, chunk), chunk)
        p = pb[rows, :].astype(F32)
        dp = scores[rows, :]
        delta = jnp.sum(p * dp, axis=-1, keepdims=True)
        ds[rows, :] = (p * (dp - delta)).astype(BF16)

    def norm_back(raw, gain, grad):
        r = scale_of(raw)
        inner = grad * gain
        return r * inner - raw * (r * r * r * jnp.mean(raw * inner, axis=-1, keepdims=True))

    dkh = dot(ds[...], qh[...], 0, 0)
    dvh = dot(pb[...], datt[...], 0, 0)
    for s in range(BACK + 1):
        rows = slice(s * SLAB, s * SLAB + SLAB)
        dk = norm_back(kvwin[rows, 0:HD].astype(F32), kgain, dkh[rows])
        if s == BACK:
            dkv_own[:, 0:HD] = dk
            dkv_own[:, HD:] = dvh[rows]
        else:
            dkv[s, :, 0:HD] = dk.astype(BF16)
            dkv[s, :, HD:] = dvh[rows].astype(BF16)

    def dk_copy(i):
        return remote(
            dkv.at[BACK - i], dkv_in.at[i - 1], s_dk.at[i - 1], r_dk.at[i - 1], back_row(i), col,
        )

    for i in range(1, BACK + 1):
        dk_copy(i).start()

    dqh = dot(ds[...], kh[...], 1, 0)
    for h in range(2):
        lanes = slice(HD * h, HD * h + HD)
        dqkv[:, lanes] = norm_back(
            q_raw[:, lanes].astype(F32), qgain, dqh[SLAB * h : SLAB * h + SLAB]
        ).astype(BF16)

    sum_second(0)
    reduce_middle(OUT)

    for i in range(1, BACK + 1):
        dk_copy(i).wait_recv()
    total = dkv_own[...]
    for i in range(BACK):
        total = total + dkv_in[i].astype(F32)
    dqkv[:, 256:512] = total.astype(BF16)

    for k in (2, 1, 3, 0):
        @pl.loop(0, 2)
        def _(cc):
            c = 2 * xs[k] + cc
            g_qkv[c] = dot(tok[c], dqkv[...], 0, 0).astype(BF16)

        if k == 2:
            reduce_start(QKV)

    @pl.loop(0, 8)
    def _(c):
        zbuf[c] = dot(dqkv[...], w_qkv[c], 1, 1).astype(BF16)

    sum_start(1)
    sum_second(1)
    reduce_middle(QKV)

    sum_last(0, layer_out)
    reduce_wait(OUT)
    for q in (0, 1):
        go_out[:, 256 * q : 256 * q + 256] = reduce_last(OUT, q)[0:OWN]
    sum_last(1, input_grad)
    reduce_wait(QKV)
    for q in (0, 1):
        done = reduce_last(QKV, q)
        gq_out[:, 256 * q : 256 * q + 256] = done[0:OWN, 0:256]
        gk_out[:, 128 * q : 128 * q + 128] = done[0:OWN, 256:384]
        gv_out[:, 128 * q : 128 * q + 128] = done[0:OWN, 384:512]

    for a in (QKV, OUT):
        @pl.loop(1, 8)
        def _(d):
            z_copy(a, d, z, lax.rem(z + d, NZ)).wait_send()
            rz_copy(a, d, z).wait_send()

        @pl.loop(0, 8)
        def _(i):
            for side in (0, 1):
                xf_copy(a, i, side, x).wait_send()
                xh_copy(a, i, side, xs[3] if side == 0 else xs[1]).wait_send()
                rl_copy(a, i, side).wait_send()
                fl_copy(a, i, side).wait_send()

    for t in (0, 1):
        @pl.loop(1, 8)
        def _(e):
            t_copy(t, e).wait_send()
            yy_copy(t, e).wait_send()

        @pl.loop(0, 8)
        def _(e):
            sib_copy(t, e, core).wait_send()

        @pl.loop(0, NY)
        def _(yy):
            ys_copy(t, yy).wait_send()

    for i in range(1, BACK + 1):
        kv_copy(i).wait_send()
        dk_copy(i).wait_send()


def shards(tokens, w_query, w_key, w_value, w_output, query_gain, key_gain, cotangent):
    vmem = lambda *shape, dtype=BF16: pltpu.VMEM(shape, dtype)
    dma = lambda *shape: pltpu.SemaphoreType.DMA(shape)
    spec = pl.BlockSpec(memory_space=pltpu.VMEM)
    scratch = [
        vmem(4 * OWN, BLOCK),
        vmem(8, SLAB, BLOCK), vmem(8, SLAB, BLOCK),
        vmem(2, SENT, 512), vmem(2, SENT, 256),
        vmem(8, BLOCK, 512), vmem(8, BLOCK, 256),
        vmem(8, BLOCK, 512), vmem(8, BLOCK, 256),
        vmem(SLAB, 512, dtype=F32), vmem(SLAB, 256), vmem(2 * SLAB, HD), vmem(KEYS, HD),
        vmem(KEYS, 2 * HD), vmem(2 * SLAB, KEYS, dtype=F32), vmem(2 * SLAB, KEYS),
        vmem(2 * SLAB, KEYS), vmem(SLAB, 256), vmem(2 * SLAB, HD),
        vmem(BACK, SLAB, 256), vmem(SLAB, 256, dtype=F32), vmem(BACK, SLAB, 256), vmem(SLAB, 512),
        vmem(8, SLAB, BLOCK), vmem(NY, SLAB, BLOCK), vmem(8, TOK, BLOCK),
        vmem(8, SLAB, BLOCK), vmem(NY, SLAB, BLOCK), vmem(8, TOK, BLOCK),
        vmem(2, 8, SENT, 256), vmem(2, 8, SENT, 128),
        vmem(2, 8, SENT, 512), vmem(2, 8, SENT, 256),
        vmem(8, SENT, 512), vmem(8, SENT, 256),
        dma(2),
        dma(2, 8), dma(2, 8),
        dma(2, 2, 8), dma(2, 2, 8),
        dma(2, 2, 8), dma(2, 2, 8),
        dma(2, 8), dma(2, 8),
        dma(2, 8), dma(2, 8),
        dma(BACK), dma(BACK), dma(BACK), dma(BACK),
        dma(2, 2, 8), dma(2, 2, 8),
        dma(2, 2, 8), dma(2, 2, 8),
        dma(2, 8), dma(2, 8),
        dma(2, NY), dma(2, NY),
        dma(2, 8), dma(2, 8),
    ]
    outs = [
        jax.ShapeDtypeStruct(tokens.shape, BF16),
        jax.ShapeDtypeStruct(tokens.shape, BF16),
        jax.ShapeDtypeStruct(w_query.shape, BF16),
        jax.ShapeDtypeStruct(w_key.shape, BF16),
        jax.ShapeDtypeStruct(w_value.shape, BF16),
        jax.ShapeDtypeStruct(w_output.shape[::-1], BF16),
    ]
    layer_out, input_grad, gq, gk, gv, go = pl.pallas_call(
        kernel,
        out_shape=outs,
        in_specs=[spec] * 8,
        out_specs=[spec] * 6,
        scratch_shapes=scratch,
        compiler_params=pltpu.CompilerParams(
            collective_id=0, has_side_effects=True, vmem_limit_bytes=64 * 1024 * 1024 - 65536
        ),
    )(
        tokens, cotangent, w_query, w_key, w_value, w_output.T,
        query_gain.reshape(1, HD), key_gain.reshape(1, HD),
    )
    return layer_out, input_grad, gq, gk, gv, go.T


def solution(mesh):
    in_specs = (
        P("row", "col"), P("row", "col"), P("row", "col"), P("row", "col"), P("col", "row"),
        P(), P(), P("row", "col"),
    )
    out_specs = (
        P("row", "col"), P("row", "col"), P("row", "col"), P("row", "col"), P("row", "col"),
        P("col", "row"),
    )
    return jax.shard_map(shards, mesh=mesh, in_specs=in_specs, out_specs=out_specs, check_vma=False)
```

time: 1040 us -> 231 us (0.22)
  waiting for transfers between devices: 891 us -> 0 us
  Pallas kernels: 0 us -> 220 us
  matrix products: 53 us -> 0 us
  starting transfers between devices: 37.4 us -> 0 us
  local copies, waits for them, and re-layouts: 28.9 us -> 8.18 us
  between operations: 14.7 us -> 0.66 us
  other arithmetic: 11.4 us -> 0 us
    all_gather x6 -> x0, waiting for transfers between devices: 329 us -> none  [the longest x1 86.2 us: shards(): full_output = lax.all_gather(w_output, 'row', axis=1, tiled=True)]
    reduce_scatter x3 -> x0, waiting for transfers between devices: 301 us -> none  [the longest x1 229 us: shards(): lax.psum_scatter(dot_first(attended, grad_rows).astype(jnp.bfloat16), 'ro...]
    unnamed x11 -> x0, waiting for transfers between devices: 225 us -> none
    pallas_call x0 -> x1, Pallas kernels: none -> 220 us  [shards(): pl.pallas_call(kernel, out_shape=outs, in_specs=[spec] * 8, out_specs=[sp...]
    dot_general x15 -> x0, matrix products: 49.1 us -> none  [the longest x4 11.7 us: dot_last(): lax.dot_general(left_side, right_side, (((1,), (1,)), ((), ())), preferre...]
    ppermute x16 -> x0, starting transfers between devices: 37 us -> none  [from_behind(): lax.ppermute(value, axis, [(source, source + steps) for source in range(i...]
    ppermute x16 -> x0, waiting for transfers between devices: 35.9 us -> none  [from_behind(): lax.ppermute(value, axis, [(source, source + steps) for source in range(i...]
  transfers between devices with their start and end apart: 26 -> 0, of which waited for: 19 -> 0; matrix products, arithmetic and copies ran while one was open for 4% -> 0% of each run, Pallas kernels for 0% -> 0%
where the time goes in v1:
time: 231 us; the launch traced here: 228 us
  Pallas kernels  220 us (95%)
  local copies, waits for them, and re-layouts  8.18 us (4%)
    pallas_call x1, Pallas kernels, shards(): pl.pallas_call(kernel, out_shape=outs, in_specs=[spec] * 8, out_specs=[sp...  220 us
    unnamed x20, local copies, waits for them, and re-layouts  8.18 us

profile of v1, /device:TPU:1, one launch (start us, length us, event | category | flops | bytes accessed | tf_op | source)
XLA Modules:
  0.0 228.5 jit_solution(15705374542378755659)
XLA Ops:
  0.6 0.0 copy-start.1
  0.6 1.8 copy.14.tok_in
  2.4 0.0 copy-done.1
  2.4 0.8 copy.15.cot_in
  3.2 219.6 %shard_map.127 = (bf16[128,672]{1,0:T(8,128)(2,1)}, bf16[128,672]{1,0:T(8,128)(2,1)}, bf16[168,512]{1,0:T(8,128)(2,1)}, bf16[168,256]{1,0:T(8,128)(2,1)}, bf16[1...) custom-call(bf16[128,672]{1,0:T(8,128)(2,1)} %copy.14.tok_in, bf16[128,672]{1,0:T(8,128)(2,1)} %copy.15.cot_in, ...), custom_call_target="tpu_custom_call" | custom-call | tf_op jit(solution)/shard_map/pallas_call | solution.py:639
  222.9 0.0 copy-start
  222.9 1.8 copy.16
  224.7 0.0 copy-done
  224.7 0.0 copy-start.3
  224.7 0.8 copy.17
  225.5 0.1 copy-done.3
  225.6 0.0 copy-start.5
  225.6 0.0 copy-start.4
  225.6 0.7 copy.22
  226.3 0.3 copy-done.5
  226.5 0.0 copy-start.2
  226.5 0.6 copy.23
  227.2 0.0 copy-done.4
  227.2 0.6 copy.24
  227.8 0.0 copy-done.2
  227.8 0.7 copy.25
Async XLA Ops:
  0.6 1.8 copy-start.1
  222.9 1.8 copy-start
  224.7 0.9 copy-start.3
  225.6 0.9 copy-start.5
  225.6 1.6 copy-start.4
  226.5 1.3 copy-start.2

commit v2 on v0

v2 whole, which is shorter than its diff:
```python
import jax
import jax.numpy as jnp
from jax import lax
from jax.experimental import pallas as pl
from jax.experimental.pallas import tpu as pltpu
from jax.sharding import PartitionSpec as P

BF16 = jnp.bfloat16
F32 = jnp.float32

NX, NZ, NY = 4, 8, 4

OWN, SENT, PITCH, BLOCK = 168, 176, 192, 768
TOK = 128
SUPER = 1024
SLAB = 256
HD = 128
BACK = 4
KEYS = (BACK + 1) * SLAB
WINDOW = 1024
KV, Q, OUT = 0, 1, 2
ATT, DQ, DKV = 0, 1, 2
query_scalar = 168.0
epsilon = 1e-06


def dot(a, b, ca, cb):
    return lax.dot_general(a, b, (((ca,), (cb,)), ((), ())), preferred_element_type=F32)


def ring(a, n):
    return lax.rem(a + n, n)


def spread():
    i = lax.broadcasted_iota(jnp.int32, (4 * OWN, BLOCK), 0)
    j = lax.broadcasted_iota(jnp.int32, (4 * OWN, BLOCK), 1)
    group = (
        (i >= OWN).astype(jnp.int32)
        + (i >= 2 * OWN).astype(jnp.int32)
        + (i >= 3 * OWN).astype(jnp.int32)
    )
    return (j == i + (PITCH - OWN) * group).astype(F32).astype(BF16)


def kernel(
    tok_in, cot_in, wq_in, wk_in, wv_in, wo_in, qg_ref, kg_ref,
    layer_out, input_grad, gq_out, gk_out, gv_out, go_out,
    place, piece, slabs, w, g, part, sum_half, sum_full, gath,
    q_raw, qh, kh, kvwin, scores, pb, ds, datt, dkv, dkv_own, dkv_in,
    ypart, ysib, yrecv, last, relay, full,
    s_xf, r_xf, s_xh, r_xh, s_p, r_p, s_y, r_y, s_s, r_s, s_l,
    s_rs, r_rs, s_ag, r_ag, s_ah, r_ah, s_kv, r_kv, s_dk, r_dk,
    s_rl, r_rl, s_fl, r_fl, s_os, r_os, s_oy, r_oy, s_oz, r_oz,
):
    row = lax.axis_index("row")
    col = lax.axis_index("col")
    x, z = lax.div(row, NZ), lax.rem(row, NZ)
    y, core = lax.div(col, 2), lax.rem(col, 2)
    head, quarter = lax.div(z, 4), lax.rem(z, 4)
    collects = core == head
    xs = [ring(x + d, NX) for d in range(NX)]
    zs = [ring(z + d, NZ) for d in range(NZ)]
    ys = [ring(y + d, NY) for d in range(NY)]
    sibling = col + 1 - 2 * core
    place_in_ring = 4 * x + quarter

    def remote(src, dst, ssem, rsem, to_row, to_col):
        return pltpu.make_async_remote_copy(
            src_ref=src, dst_ref=dst, send_sem=ssem, recv_sem=rsem,
            device_id={"row": to_row, "col": to_col}, device_id_type=pl.DeviceIdType.MESH,
        )

    def token_row(i):
        at = lax.rem(place_in_ring + 16 + i, 16)
        return lax.div(at, 4) * NZ + 4 * head + lax.rem(at, 4)

    def x_row(side):
        return (xs[1] if side == 0 else xs[3]) * NZ + z

    def z_row(side):
        return x * NZ + (zs[1] if side == 0 else zs[7])

    barrier = pltpu.get_barrier_semaphore()

    def greet(to_row, to_col):
        pl.semaphore_signal(
            barrier, inc=1, device_id={"row": to_row, "col": to_col},
            device_id_type=pl.DeviceIdType.MESH,
        )

    for d in range(1, NZ):
        greet(x * NZ + zs[d], col)
    for d in range(1, NY):
        greet(row, 2 * ys[d] + core)
    for i in range(1, BACK + 1):
        greet(token_row(i), col)
        greet(token_row(-i), col)
    greet(row, sibling)
    greet(x_row(0), col)
    greet(x_row(1), col)

    def rows_at(i):
        return pl.ds(pl.multiple_of(PITCH * i, 16), SENT)

    own_rows = rows_at(x)
    for u in (KV, Q, OUT):
        w[u, pl.ds(pl.multiple_of(PITCH * x + 160, 16), 16), :] = jnp.zeros((16, 512), BF16)
    weight_rows = pl.ds(pl.multiple_of(PITCH * x, 16), OWN)
    for h in (0, 1):
        w[KV, weight_rows, 256 * h : 256 * h + 128] = wk_in[:, 128 * h : 128 * h + 128]
        w[KV, weight_rows, 256 * h + 128 : 256 * h + 256] = wv_in[:, 128 * h : 128 * h + 128]
    w[Q, weight_rows, :] = wq_in[...]
    w[OUT, weight_rows, :] = wo_in[...]

    pl.semaphore_wait(barrier, 21)

    def xf_copy(u, side, xx):
        slot = w.at[u, rows_at(xx)]
        return remote(slot, slot, s_xf.at[u, side], r_xf.at[u, side], x_row(side), col)

    def xh_copy(u, side, xx):
        slot = w.at[u, rows_at(xx), pl.ds(256 * side, 256)]
        return remote(slot, slot, s_xh.at[u, side], r_xh.at[u, side], x_row(side), col)

    def weight_start(u):
        xf_copy(u, 0, x).start()
        xf_copy(u, 1, x).start()

    def weight_forward(u):
        xf_copy(u, 0, xs[3]).wait_recv()
        xh_copy(u, 0, xs[3]).start()
        xf_copy(u, 1, xs[1]).wait_recv()
        xh_copy(u, 1, xs[1]).start()

    def weight_wait(u):
        xh_copy(u, 0, xs[2]).wait_recv()
        xh_copy(u, 1, xs[2]).wait_recv()

    for u in (KV, Q, OUT):
        weight_start(u)

    def lanes_at(i):
        return pl.ds(pl.multiple_of(TOK * i, TOK), TOK)

    def piece_copy(t, j, zt):
        return remote(
            piece.at[t, pl.ds(pl.multiple_of(PITCH * j, 16), SENT)],
            slabs.at[t, rows_at(y), lanes_at(z)],
            s_p.at[t, j], r_p.at[t, z], x * NZ + zt, col,
        )

    def piece_recv(t, zf):
        slot = slabs.at[t, rows_at(y), lanes_at(zf)]
        return remote(slot, slot, s_p.at[t, 0], r_p.at[t, zf], x * NZ + zf, col)

    def piece_own(t):
        return pltpu.make_async_copy(
            piece.at[t, pl.ds(pl.multiple_of(PITCH * quarter, 16), SENT)],
            slabs.at[t, rows_at(y), lanes_at(z)], s_l.at[t],
        )

    def piece_start(t):
        @pl.loop(0, 4)
        def _(i):
            j = lax.rem(quarter + 1 + i, 4)
            zt = 4 * core + j

            @pl.when(zt != z)
            def _():
                piece_copy(t, j, zt).start()

        @pl.when(collects)
        def _():
            piece_own(t).start()

    def slab_copy(t, dy, yy):
        slot = slabs.at[t, rows_at(yy)]
        return remote(slot, slot, s_y.at[t, dy], r_y.at[t, dy], row, 2 * ys[dy] + core)

    def share_copy(t, dy):
        slot = slabs.at[t, rows_at(ys[(NY - dy) % NY])]
        return remote(slot, slot, s_s.at[t, dy], r_s.at[t, dy], row, sibling)

    def collect(t):
        @pl.when(collects)
        def _():
            piece_own(t).wait()
            for d in range(1, NZ):
                piece_recv(t, zs[d]).wait_recv()
            for dy in (1, 3, 2):
                slab_copy(t, dy, y).start()
            share_copy(t, 0).start()

    def share(t):
        @pl.when(collects)
        def _():
            for dy in (1, 3, 2):
                slab_copy(t, dy, ys[NY - dy]).wait_recv()
                share_copy(t, dy).start()

        @pl.when(jnp.logical_not(collects))
        def _():
            for dy in range(NY):
                share_copy(t, dy).wait_recv()

    place[...] = spread()
    piece[0] = dot(place[...], tok_in[...], 0, 1).astype(BF16)
    piece_start(0)
    piece[1] = dot(place[...], cot_in[...], 0, 1).astype(BF16)
    piece_start(1)
    for j in range(4):
        gap = slice(PITCH * j + SENT, PITCH * (j + 1))
        for u in (KV, Q, OUT):
            w[u, gap, :] = jnp.zeros((PITCH - SENT, 512), BF16)
        for t in (0, 1):
            slabs[t, gap, :] = jnp.zeros((PITCH - SENT, SUPER), BF16)
            last[t, gap, :] = jnp.zeros((PITCH - SENT, TOK), BF16)

    def rs_copy(u, step, side):
        if step == 1:
            rows = pl.ds(TOK * side, TOK)
            src, dst = part.at[u, zs[4], rows], sum_half.at[u, side]
        else:
            to = zs[5 - step] if side == 0 else zs[3 + step]
            src, dst = part.at[u, to], sum_full.at[u, side, step - 2]
        return remote(
            src, dst, s_rs.at[u, side, step - 1], r_rs.at[u, side, step - 1], z_row(side), col
        )

    def rs_step(u, step):
        for side in (0, 1):
            if step > 1:
                rs_copy(u, step - 1, side).wait_recv()
                to = zs[5 - step] if side == 0 else zs[3 + step]
                if step == 2:
                    rows = slice(TOK * side, TOK * side + TOK)
                    part[u, to, rows] = (
                        part[u, to, rows].astype(F32) + sum_half[u, side].astype(F32)
                    ).astype(BF16)
                else:
                    part[u, to] = (
                        part[u, to].astype(F32) + sum_full[u, side, step - 3].astype(F32)
                    ).astype(BF16)
            rs_copy(u, step, side).start()

    def rs_total(u):
        rs_copy(u, 4, 0).wait_recv()
        rs_copy(u, 4, 1).wait_recv()
        return (
            part[u, z].astype(F32)
            + sum_full[u, 0, 2].astype(F32)
            + sum_full[u, 1, 2].astype(F32)
        ).astype(BF16)

    def ag_copy(v, step, side, sending):
        back = step - 1 if sending else step
        slot = zs[(NZ - back) % NZ] if side == 0 else zs[back]
        if step == 4:
            rows = pl.ds(TOK * side, TOK)
            block = gath.at[v, slot, rows]
        else:
            block = gath.at[v, slot]
        return remote(
            block, block, s_ag.at[v, side, step - 1], r_ag.at[v, side, step - 1], z_row(side), col
        )

    def ag_step(v, step):
        for side in (0, 1):
            if step > 1:
                ag_copy(v, step - 1, side, False).wait_recv()
            if step < 5:
                ag_copy(v, step, side, True).start()

    def gathered(v, h):
        return gath[v, 4 * h : 4 * h + 4].reshape(SUPER, SLAB)

    def project(u, t):
        for h in (0, 1):
            part[u, 4 * h : 4 * h + 4] = (
                dot(slabs[t], w[u, :, 256 * h : 256 * h + 256], 0, 0)
                .astype(BF16)
                .reshape(4, SLAB, SLAB)
            )

    weight_forward(KV)
    collect(0)
    weight_forward(Q)
    share(0)
    weight_wait(KV)
    project(KV, 0)
    rs_step(KV, 1)
    weight_wait(Q)
    project(Q, 0)
    rs_step(Q, 1)
    collect(1)
    weight_forward(OUT)
    rs_step(KV, 2)
    rs_step(Q, 2)
    rs_step(KV, 3)
    share(1)
    weight_wait(OUT)
    rs_step(Q, 3)
    rs_step(KV, 4)
    project(OUT, 1)
    rs_step(OUT, 1)
    rs_step(Q, 4)

    own_keys = pl.ds(BACK * SLAB, SLAB)
    kvwin[own_keys, :] = rs_total(KV)

    def kv_copy(i):
        return remote(
            kvwin.at[own_keys], kvwin.at[pl.ds((BACK - i) * SLAB, SLAB)],
            s_kv.at[i - 1], r_kv.at[i - 1], token_row(i), col,
        )

    for i in range(1, BACK + 1):
        kv_copy(i).start()
    rs_step(OUT, 2)

    def scale_of(values):
        return lax.rsqrt(jnp.mean(values * values, axis=-1, keepdims=True) + epsilon)

    qgain = qg_ref[...] * query_scalar ** (-0.5)
    kgain = kg_ref[...]
    q_raw[...] = rs_total(Q)
    for r in range(2):
        q = q_raw[:, HD * r : HD * r + HD].astype(F32)
        qh[SLAB * r : SLAB * r + SLAB, :] = (q * scale_of(q) * qgain).astype(BF16)
    rs_step(OUT, 3)

    for i in range(1, BACK + 1):
        kv_copy(i).wait_recv()


    @pl.loop(0, BACK + 1)
    def _(s):
        rows = pl.ds(pl.multiple_of(s * SLAB, SLAB), SLAB)
        k = kvwin[rows, 0:HD].astype(F32)
        kh[rows, :] = (k * scale_of(k) * kgain).astype(BF16)

    scores[...] = dot(qh[...], kh[...], 1, 1)
    rs_step(OUT, 4)
    chunk = 32
    first_key = WINDOW - SLAB * place_in_ring

    @pl.loop(0, 2 * SLAB // chunk)
    def _(n):
        rows = pl.ds(pl.multiple_of(n * chunk, chunk), chunk)
        t0 = lax.rem(n, SLAB // chunk) * chunk
        t = t0 + lax.broadcasted_iota(jnp.int32, (chunk, 1), 0)
        key = lax.broadcasted_iota(jnp.int32, (chunk, KEYS), 1)
        allowed = (key <= t + WINDOW) & (key >= jnp.maximum(t + 1, first_key))
        s = jnp.where(allowed, scores[rows, :], -1e30)
        e = jnp.exp(s - jnp.max(s, axis=-1, keepdims=True))
        pb[rows, :] = (e * (1.0 / jnp.sum(e, axis=-1, keepdims=True))).astype(BF16)

    blended = dot(pb[...], kvwin[:, HD:], 1, 0).astype(BF16)
    for r in range(2):
        gath[ATT, z, :, HD * r : HD * r + HD] = blended[SLAB * r : SLAB * r + SLAB]
    ag_step(ATT, 1)

    total = rs_total(OUT)
    for r in range(2):
        datt[SLAB * r : SLAB * r + SLAB, :] = total[:, HD * r : HD * r + HD]

    scores[...] = dot(datt[...], kvwin[:, HD:], 1, 1)
    ag_step(ATT, 2)

    @pl.loop(0, 2 * SLAB // chunk)
    def _(n):
        rows = pl.ds(pl.multiple_of(n * chunk, chunk), chunk)
        p = pb[rows, :].astype(F32)
        dp = scores[rows, :]
        delta = jnp.sum(p * dp, axis=-1, keepdims=True)
        ds[rows, :] = (p * (dp - delta)).astype(BF16)

    ag_step(ATT, 3)

    def norm_back(raw, gain, grad):
        r = scale_of(raw)
        inner = grad * gain
        return r * inner - raw * (r * r * r * jnp.mean(raw * inner, axis=-1, keepdims=True))

    dkh = dot(ds[...], qh[...], 0, 0)
    dvh = dot(pb[...], datt[...], 0, 0)
    for s in range(BACK + 1):
        rows = slice(s * SLAB, s * SLAB + SLAB)
        dk = norm_back(kvwin[rows, 0:HD].astype(F32), kgain, dkh[rows])
        if s == BACK:
            dkv_own[:, 0:HD] = dk
            dkv_own[:, HD:] = dvh[rows]
        else:
            dkv[s, :, 0:HD] = dk.astype(BF16)
            dkv[s, :, HD:] = dvh[rows].astype(BF16)

    def dk_copy(i):
        return remote(
            dkv.at[BACK - i], dkv_in.at[i - 1], s_dk.at[i - 1], r_dk.at[i - 1], token_row(-i), col
        )

    for i in range(1, BACK + 1):
        dk_copy(i).start()
    ag_step(ATT, 4)

    dqh = dot(ds[...], kh[...], 1, 0)
    for r in range(2):
        lanes = slice(HD * r, HD * r + HD)
        gath[DQ, z, :, lanes] = norm_back(
            q_raw[:, lanes].astype(F32), qgain, dqh[SLAB * r : SLAB * r + SLAB]
        ).astype(BF16)
    ag_step(DQ, 1)
    ag_step(ATT, 5)

    def rl_copy(u, side):
        return remote(
            g.at[u, rows_at(xs[2]), pl.ds(256 * side, 256)], relay.at[u, side],
            s_rl.at[u, side], r_rl.at[u, side], x_row(side), col,
        )

    def fl_copy(u, side):
        return remote(
            g.at[u, rows_at(xs[1] if side == 0 else xs[3])], full.at[u, side],
            s_fl.at[u, side], r_fl.at[u, side], x_row(side), col,
        )

    def grad_start(u, t, v):
        for h in (0, 1):
            g[u, :, 256 * h : 256 * h + 256] = dot(slabs[t], gathered(v, h), 1, 0).astype(BF16)
        rl_copy(u, 0).start()
        rl_copy(u, 1).start()

    def grad_middle(u):
        for side in (0, 1):
            rl_copy(u, side).wait_recv()
            rows = rows_at(xs[1] if side == 0 else xs[3])
            lanes = slice(256 * side, 256 * side + 256)
            g[u, rows, lanes] = (
                g[u, rows, lanes].astype(F32) + relay[u, side].astype(F32)
            ).astype(BF16)
            fl_copy(u, side).start()

    def grad_last(u):
        fl_copy(u, 0).wait_recv()
        fl_copy(u, 1).wait_recv()
        total = (
            g[u, own_rows, :].astype(F32)
            + full[u, 0].astype(F32)
            + full[u, 1].astype(F32)
        ).astype(BF16)
        return total[0:OWN]

    def os_copy(t, i):
        return remote(
            ypart.at[t, rows_at(i)], ysib.at[t, i], s_os.at[t, i], r_os.at[t, i], row, sibling
        )

    def oy_copy(t, dy):
        return remote(
            ypart.at[t, rows_at(ys[dy])], yrecv.at[t, dy - 1],
            s_oy.at[t, dy], r_oy.at[t, dy], row, 2 * ys[dy] + core,
        )

    def oz_copy(t, zt):
        return remote(
            ypart.at[t, rows_at(y), lanes_at(zt)], last.at[t, rows_at(quarter)],
            s_oz.at[t, zt], r_oz.at[t, quarter], x * NZ + zt, col,
        )

    def oz_recv(t, j):
        slot = last.at[t, pl.ds(PITCH * j, SENT)]
        return remote(slot, slot, s_oz.at[t, 0], r_oz.at[t, j], x * NZ + 4 * core + j, col)

    def out_start(t):
        @pl.when(jnp.logical_not(collects))
        def _():
            for i in range(NX):
                os_copy(t, i).start()

    def out_middle(t):
        @pl.when(collects)
        def _():
            for dy in (2, 1, 3, 0):
                os_copy(t, ys[dy]).wait_recv()
                rows = rows_at(ys[dy])
                ypart[t, rows, :] = (
                    ypart[t, rows, :].astype(F32) + ysib[t, ys[dy]].astype(F32)
                ).astype(BF16)
                if dy:
                    oy_copy(t, dy).start()

    def out_sum(t):
        @pl.when(collects)
        def _():
            for dy in (1, 3, 2):
                oy_copy(t, dy).wait_recv()
            rows = rows_at(y)
            total = ypart[t, rows, :].astype(F32)
            for dy in (1, 2, 3):
                total = total + yrecv[t, dy - 1].astype(F32)
            ypart[t, rows, :] = total.astype(BF16)
            for d in (4, 3, 5, 2, 6, 1, 7):
                oz_copy(t, zs[d]).start()
            last[t, rows_at(quarter), :] = ypart[t, rows, lanes_at(z)]

    def out_last(t, out):
        for j in range(4):
            @pl.when(4 * core + j != z)
            def _():
                oz_recv(t, j).wait_recv()
        out[...] = dot(last[t], place[...], 0, 1).astype(BF16)

    grad_start(OUT, 1, ATT)
    ag_step(DQ, 2)
    ypart[0] = (
        dot(w[OUT, :, 0:256], gathered(ATT, 0), 1, 1)
        + dot(w[OUT, :, 256:512], gathered(ATT, 1), 1, 1)
    ).astype(BF16)
    out_start(0)
    ag_step(DQ, 3)

    for i in range(1, BACK + 1):
        dk_copy(i).wait_recv()
    total = dkv_own[...]
    for i in range(BACK):
        total = total + dkv_in[i].astype(F32)
    gath[DKV, z] = total.astype(BF16)
    ag_step(DKV, 1)

    grad_middle(OUT)
    ag_step(DQ, 4)
    ag_step(DKV, 2)
    out_middle(0)
    ag_step(DQ, 5)
    grad_start(Q, 0, DQ)
    ag_step(DKV, 3)
    ag_step(DKV, 4)
    out_sum(0)
    grad_middle(Q)
    ag_step(DKV, 5)
    grad_start(KV, 0, DKV)
    total = (
        dot(w[Q, :, 0:256], gathered(DQ, 0), 1, 1) + dot(w[Q, :, 256:512], gathered(DQ, 1), 1, 1)
    )
    ypart[1] = (
        total
        + dot(w[KV, :, 0:256], gathered(DKV, 0), 1, 1)
        + dot(w[KV, :, 256:512], gathered(DKV, 1), 1, 1)
    ).astype(BF16)
    out_start(1)
    grad_middle(KV)
    out_middle(1)
    go_out[...] = grad_last(OUT)
    out_last(0, layer_out)
    out_sum(1)
    gq_out[...] = grad_last(Q)
    done = grad_last(KV)
    for h in (0, 1):
        gk_out[:, 128 * h : 128 * h + 128] = done[:, 256 * h : 256 * h + 128]
        gv_out[:, 128 * h : 128 * h + 128] = done[:, 256 * h + 128 : 256 * h + 256]
    out_last(1, input_grad)

    for u in (KV, Q, OUT):
        for side in (0, 1):
            xf_copy(u, side, x).wait_send()
            xh_copy(u, side, xs[3] if side == 0 else xs[1]).wait_send()
            rl_copy(u, side).wait_send()
            fl_copy(u, side).wait_send()
            for step in range(1, 5):
                rs_copy(u, step, side).wait_send()
                ag_copy(u, step, side, True).wait_send()
    for t in (0, 1):
        for j in range(4):
            @pl.when(4 * core + j != z)
            def _():
                piece_copy(t, j, 4 * core + j).wait_send()

        @pl.when(collects)
        def _():
            for dy in (1, 2, 3):
                slab_copy(t, dy, y).wait_send()
                oy_copy(t, dy).wait_send()
            for dy in range(NY):
                share_copy(t, dy).wait_send()
            for d in range(1, NZ):
                oz_copy(t, zs[d]).wait_send()

        @pl.when(jnp.logical_not(collects))
        def _():
            for i in range(NX):
                os_copy(t, i).wait_send()

    for i in range(1, BACK + 1):
        kv_copy(i).wait_send()
        dk_copy(i).wait_send()


def shards(tokens, w_query, w_key, w_value, w_output, query_gain, key_gain, cotangent):
    vmem = lambda *shape, dtype=BF16: pltpu.VMEM(shape, dtype)
    dma = lambda *shape: pltpu.SemaphoreType.DMA(shape)
    spec = pl.BlockSpec(memory_space=pltpu.VMEM)
    scratch = [
        vmem(4 * OWN, BLOCK), vmem(2, BLOCK, TOK), vmem(2, BLOCK, SUPER),
        vmem(3, BLOCK, 512), vmem(3, BLOCK, 512),
        vmem(3, NZ, SLAB, SLAB), vmem(3, 2, TOK, SLAB), vmem(3, 2, 3, SLAB, SLAB),
        vmem(3, NZ, SLAB, SLAB),
        vmem(SLAB, SLAB), vmem(2 * SLAB, HD), vmem(KEYS, HD), vmem(KEYS, 2 * HD),
        vmem(2 * SLAB, KEYS, dtype=F32), vmem(2 * SLAB, KEYS), vmem(2 * SLAB, KEYS),
        vmem(2 * SLAB, HD),
        vmem(BACK, SLAB, 256), vmem(SLAB, 256, dtype=F32), vmem(BACK, SLAB, 256),
        vmem(2, BLOCK, SUPER), vmem(2, NX, SENT, SUPER), vmem(2, 3, SENT, SUPER),
        vmem(2, BLOCK, TOK), vmem(3, 2, SENT, 256), vmem(3, 2, SENT, 512),
        dma(3, 2), dma(3, 2), dma(3, 2), dma(3, 2),
        dma(2, 4), dma(2, NZ), dma(2, NY), dma(2, NY), dma(2, NY), dma(2, NY), dma(2),
        dma(3, 2, 4), dma(3, 2, 4), dma(3, 2, 4), dma(3, 2, 4), dma(1), dma(1),
        dma(BACK), dma(BACK), dma(BACK), dma(BACK),
        dma(3, 2), dma(3, 2), dma(3, 2), dma(3, 2),
        dma(2, NX), dma(2, NX), dma(2, NY), dma(2, NY), dma(2, NZ), dma(2, 4),
    ]
    outs = [
        jax.ShapeDtypeStruct(tokens.shape, BF16),
        jax.ShapeDtypeStruct(tokens.shape, BF16),
        jax.ShapeDtypeStruct(w_query.shape, BF16),
        jax.ShapeDtypeStruct(w_key.shape, BF16),
        jax.ShapeDtypeStruct(w_value.shape, BF16),
        jax.ShapeDtypeStruct(w_output.shape[::-1], BF16),
    ]
    layer_out, input_grad, gq, gk, gv, go = pl.pallas_call(
        kernel,
        out_shape=outs,
        in_specs=[spec] * 8,
        out_specs=[spec] * 6,
        scratch_shapes=scratch,
        compiler_params=pltpu.CompilerParams(
            collective_id=0, has_side_effects=True, vmem_limit_bytes=60 * 1024 * 1024
        ),
    )(
        tokens, cotangent, w_query, w_key, w_value, w_output.T,
        query_gain.reshape(1, HD), key_gain.reshape(1, HD),
    )
    return layer_out, input_grad, gq, gk, gv, go.T


def solution(mesh):
    in_specs = (
        P("row", "col"), P("row", "col"), P("row", "col"), P("row", "col"), P("col", "row"),
        P(), P(), P("row", "col"),
    )
    out_specs = (
        P("row", "col"), P("row", "col"), P("row", "col"), P("row", "col"), P("row", "col"),
        P("col", "row"),
    )
    return jax.shard_map(shards, mesh=mesh, in_specs=in_specs, out_specs=out_specs, check_vma=False)
```

time: 1040 us -> 173 us (0.17)
  waiting for transfers between devices: 891 us -> 0 us
  Pallas kernels: 0 us -> 163 us
  matrix products: 53 us -> 0 us
  starting transfers between devices: 37.4 us -> 0 us
  local copies, waits for them, and re-layouts: 28.9 us -> 8.18 us
  between operations: 14.7 us -> 0.66 us
  other arithmetic: 11.4 us -> 0 us
    all_gather x6 -> x0, waiting for transfers between devices: 329 us -> none  [the longest x1 86.2 us: shards(): full_output = lax.all_gather(w_output, 'row', axis=1, tiled=True)]
    reduce_scatter x3 -> x0, waiting for transfers between devices: 301 us -> none  [the longest x1 229 us: shards(): lax.psum_scatter(dot_first(attended, grad_rows).astype(jnp.bfloat16), 'ro...]
    unnamed x11 -> x0, waiting for transfers between devices: 225 us -> none
    pallas_call x0 -> x1, Pallas kernels: none -> 163 us  [shards(): pl.pallas_call(kernel, out_shape=outs, in_specs=[spec] * 8, out_specs=[sp...]
    dot_general x15 -> x0, matrix products: 49.1 us -> none  [the longest x4 11.7 us: dot_last(): lax.dot_general(left_side, right_side, (((1,), (1,)), ((), ())), preferre...]
    ppermute x16 -> x0, starting transfers between devices: 37 us -> none  [from_behind(): lax.ppermute(value, axis, [(source, source + steps) for source in range(i...]
    ppermute x16 -> x0, waiting for transfers between devices: 35.9 us -> none  [from_behind(): lax.ppermute(value, axis, [(source, source + steps) for source in range(i...]
  transfers between devices with their start and end apart: 26 -> 0, of which waited for: 19 -> 0; matrix products, arithmetic and copies ran while one was open for 4% -> 0% of each run, Pallas kernels for 0% -> 0%
where the time goes in v2:
time: 173 us; the launch traced here: 171 us
  Pallas kernels  163 us (94%)
  local copies, waits for them, and re-layouts  8.18 us (5%)
    pallas_call x1, Pallas kernels, shards(): pl.pallas_call(kernel, out_shape=outs, in_specs=[spec] * 8, out_specs=[sp...  163 us
    unnamed x20, local copies, waits for them, and re-layouts  8.18 us

profile of v2, /device:TPU:1, one launch (start us, length us, event | category | flops | bytes accessed | tf_op | source)
XLA Modules:
  0.0 171.4 jit_solution(5917672056424172089)
XLA Ops:
  0.6 0.0 copy-start.1
  0.6 1.8 %copy.14.tok_in = bf16[128,672]{1,0:T(8,128)(2,1)} copy(bf16[128,672]{0,1:T(8,128)(2,1)} %param.8) | data formatting | bytes 344064 | tf_op args[0]
  2.4 0.0 copy-done.1
  2.4 0.8 copy.15.cot_in
  3.2 162.5 %shard_map.127 = (bf16[128,672]{1,0:T(8,128)(2,1)}, bf16[128,672]{1,0:T(8,128)(2,1)}, bf16[168,512]{1,0:T(8,128)(2,1)}, bf16[168,256]{1,0:T(8,128)(2,1)}, bf16[1...) custom-call(bf16[128,672]{1,0:T(8,128)(2,1)} %copy.14.tok_in, bf16[128,672]{1,0:T(8,128)(2,1)} %copy.15.cot_in, ...), custom_call_target="tpu_custom_call" | custom-call | tf_op jit(solution)/shard_map/pallas_call | solution.py:629
  165.8 0.0 copy-start
  165.8 1.8 %copy.16 = bf16[128,672]{0,1:T(8,128)(2,1)} copy(bf16[128,672]{1,0:T(8,128)(2,1)} %get-tuple-element.18) | data formatting | bytes 344064
  167.5 0.0 copy-done
  167.5 0.0 copy-start.3
  167.5 0.8 copy.17
  168.4 0.1 copy-done.3
  168.5 0.0 copy-start.5
  168.5 0.0 copy-start.4
  168.5 0.7 copy.22
  169.1 0.3 copy-done.5
  169.4 0.0 copy-start.2
  169.4 0.6 copy.23
  170.0 0.0 copy-done.4
  170.0 0.6 copy.24
  170.7 0.0 copy-done.2
  170.7 0.7 copy.25
Async XLA Ops:
  0.6 1.8 %copy-start.1 = (bf16[128,672]{0,1:T(8,128)(2,1)S(1)}, bf16[128,672]{0,1:T(8,128)(2,1)}, u32[]{:S(2)}) copy-start(bf16[128,672]{0,1:T(8,128)(2,1)} %param.15) | copy-start | bytes 516100
  165.8 1.8 %copy-start = (bf16[128,672]{1,0:T(8,128)(2,1)S(1)}, bf16[128,672]{1,0:T(8,128)(2,1)}, u32[]{:S(2)}) copy-start(bf16[128,672]{1,0:T(8,128)(2,1)} %get-tuple-element.19) | copy-start | bytes 516100
  167.5 0.9 copy-start.3
  168.5 0.9 copy-start.5
  168.5 1.6 copy-start.4
  169.4 1.3 copy-start.2

commit v3 on v2

--- a/solution.py
+++ b/solution.py
@@ -32,25 +32,14 @@
     return lax.rem(a + n, n)
 
 
-def spread():
-    i = lax.broadcasted_iota(jnp.int32, (4 * OWN, BLOCK), 0)
-    j = lax.broadcasted_iota(jnp.int32, (4 * OWN, BLOCK), 1)
-    group = (
-        (i >= OWN).astype(jnp.int32)
-        + (i >= 2 * OWN).astype(jnp.int32)
-        + (i >= 3 * OWN).astype(jnp.int32)
-    )
-    return (j == i + (PITCH - OWN) * group).astype(F32).astype(BF16)
-
-
 def kernel(
     tok_in, cot_in, wq_in, wk_in, wv_in, wo_in, qg_ref, kg_ref,
     layer_out, input_grad, gq_out, gk_out, gv_out, go_out,
-    place, piece, slabs, w, g, part, sum_half, sum_full, gath,
+    piece, slabs, w, g, part, sum_half, sum_full, gath,
     q_raw, qh, kh, kvwin, scores, pb, ds, datt, dkv, dkv_own, dkv_in,
-    ypart, ysib, yrecv, last, relay, full,
-    s_xf, r_xf, s_xh, r_xh, s_p, r_p, s_y, r_y, s_s, r_s, s_l,
-    s_rs, r_rs, s_ag, r_ag, s_ah, r_ah, s_kv, r_kv, s_dk, r_dk,
+    ypart, rest, ysib, yrecv, last, relay, full,
+    s_xf, r_xf, s_xh, r_xh, s_p, r_p, s_y, r_y, s_s, r_s,
+    s_rs, r_rs, s_ag, r_ag, s_kv, r_kv, s_dk, r_dk,
     s_rl, r_rl, s_fl, r_fl, s_os, r_os, s_oy, r_oy, s_oz, r_oz,
 ):
     row = lax.axis_index("row")
@@ -58,7 +47,6 @@
     x, z = lax.div(row, NZ), lax.rem(row, NZ)
     y, core = lax.div(col, 2), lax.rem(col, 2)
     head, quarter = lax.div(z, 4), lax.rem(z, 4)
-    collects = core == head
     xs = [ring(x + d, NX) for d in range(NX)]
     zs = [ring(z + d, NZ) for d in range(NZ)]
     ys = [ring(y + d, NY) for d in range(NY)]
@@ -89,8 +77,14 @@
             device_id_type=pl.DeviceIdType.MESH,
         )
 
-    for d in range(1, NZ):
-        greet(x * NZ + zs[d], col)
+    at_home = core == head
+    for j in range(4):
+        @pl.when(4 * core + j != z)
+        def _():
+            greet(x * NZ + 4 * core + j, 2 * y + head)
+
+    greet(z_row(0), col)
+    greet(z_row(1), col)
     for d in range(1, NY):
         greet(row, 2 * ys[d] + core)
     for i in range(1, BACK + 1):
@@ -113,7 +107,7 @@
     w[Q, weight_rows, :] = wq_in[...]
     w[OUT, weight_rows, :] = wo_in[...]
 
-    pl.semaphore_wait(barrier, 21)
+    pl.semaphore_wait(barrier, 20 - at_home.astype(jnp.int32))
 
     def xf_copy(u, side, xx):
         slot = w.at[u, rows_at(xx)]
@@ -137,85 +131,73 @@
         xh_copy(u, 0, xs[2]).wait_recv()
         xh_copy(u, 1, xs[2]).wait_recv()
 
-    for u in (KV, Q, OUT):
-        weight_start(u)
+    weight_start(KV)
 
     def lanes_at(i):
         return pl.ds(pl.multiple_of(TOK * i, TOK), TOK)
 
-    def piece_copy(t, j, zt):
-        return remote(
-            piece.at[t, pl.ds(pl.multiple_of(PITCH * j, 16), SENT)],
-            slabs.at[t, rows_at(y), lanes_at(z)],
-            s_p.at[t, j], r_p.at[t, z], x * NZ + zt, col,
-        )
-
-    def piece_recv(t, zf):
-        slot = slabs.at[t, rows_at(y), lanes_at(zf)]
-        return remote(slot, slot, s_p.at[t, 0], r_p.at[t, zf], x * NZ + zf, col)
-
-    def piece_own(t):
-        return pltpu.make_async_copy(
-            piece.at[t, pl.ds(pl.multiple_of(PITCH * quarter, 16), SENT)],
-            slabs.at[t, rows_at(y), lanes_at(z)], s_l.at[t],
+    def half_at(c):
+        return pl.ds(pl.multiple_of(512 * c, 512), 512)
+
+    def piece_copy(t, j):
+        return remote(
+            piece.at[t, pl.ds(PITCH * j, SENT)], slabs.at[t, rows_at(y), lanes_at(z)],
+            s_p.at[t, j], r_p.at[t, quarter], x * NZ + 4 * core + j, 2 * y + head,
+        )
+
+    def piece_recv(t, j):
+        slot = slabs.at[t, rows_at(y), lanes_at(4 * core + j)]
+        return remote(
+            slot, slot, s_p.at[t, j], r_p.at[t, j], x * NZ + 4 * core + j, 2 * y + head
         )
 
     def piece_start(t):
-        @pl.loop(0, 4)
-        def _(i):
-            j = lax.rem(quarter + 1 + i, 4)
-            zt = 4 * core + j
-
-            @pl.when(zt != z)
+        for j in range(4):
+            @pl.when(4 * core + j != z)
             def _():
-                piece_copy(t, j, zt).start()
-
-        @pl.when(collects)
-        def _():
-            piece_own(t).start()
+                piece_copy(t, j).start()
+
+            @pl.when(4 * core + j == z)
+            def _():
+                slabs[t, rows_at(y), lanes_at(z)] = piece[t, PITCH * j : PITCH * j + SENT]
 
     def slab_copy(t, dy, yy):
-        slot = slabs.at[t, rows_at(yy)]
+        slot = slabs.at[t, rows_at(yy), half_at(core)]
         return remote(slot, slot, s_y.at[t, dy], r_y.at[t, dy], row, 2 * ys[dy] + core)
 
-    def share_copy(t, dy):
-        slot = slabs.at[t, rows_at(ys[(NY - dy) % NY])]
+    def share_copy(t, dy, cc):
+        slot = slabs.at[t, rows_at(ys[(NY - dy) % NY]), half_at(cc)]
         return remote(slot, slot, s_s.at[t, dy], r_s.at[t, dy], row, sibling)
 
     def collect(t):
-        @pl.when(collects)
-        def _():
-            piece_own(t).wait()
-            for d in range(1, NZ):
-                piece_recv(t, zs[d]).wait_recv()
-            for dy in (1, 3, 2):
-                slab_copy(t, dy, y).start()
-            share_copy(t, 0).start()
+        for j in range(4):
+            @pl.when(4 * core + j != z)
+            def _():
+                piece_recv(t, j).wait_recv()
+        for dy in (2, 1, 3):
+            slab_copy(t, dy, y).start()
+        share_copy(t, 0, core).start()
 
     def share(t):
-        @pl.when(collects)
-        def _():
-            for dy in (1, 3, 2):
-                slab_copy(t, dy, ys[NY - dy]).wait_recv()
-                share_copy(t, dy).start()
-
-        @pl.when(jnp.logical_not(collects))
-        def _():
-            for dy in range(NY):
-                share_copy(t, dy).wait_recv()
-
-    place[...] = spread()
-    piece[0] = dot(place[...], tok_in[...], 0, 1).astype(BF16)
-    piece_start(0)
-    piece[1] = dot(place[...], cot_in[...], 0, 1).astype(BF16)
-    piece_start(1)
+        for dy in (1, 3, 2):
+            slab_copy(t, dy, ys[NY - dy]).wait_recv()
+            share_copy(t, dy, core).start()
+        for dy in (0, 1, 3, 2):
+            share_copy(t, dy, 1 - core).wait_recv()
+
+    for t, src in ((0, tok_in), (1, cot_in)):
+        for j in range(4):
+            piece[t, PITCH * j + 160 : PITCH * j + SENT] = jnp.zeros((SENT - 160, TOK), BF16)
+            piece[t, PITCH * j : PITCH * j + OWN] = src[OWN * j : OWN * j + OWN]
+        piece_start(t)
+        if t == 0:
+            weight_start(Q)
     for j in range(4):
         gap = slice(PITCH * j + SENT, PITCH * (j + 1))
         for u in (KV, Q, OUT):
             w[u, gap, :] = jnp.zeros((PITCH - SENT, 512), BF16)
         for t in (0, 1):
             slabs[t, gap, :] = jnp.zeros((PITCH - SENT, SUPER), BF16)
-            last[t, gap, :] = jnp.zeros((PITCH - SENT, TOK), BF16)
 
     def rs_copy(u, step, side):
         if step == 1:
@@ -283,29 +265,28 @@
                 .reshape(4, SLAB, SLAB)
             )
 
+    collect(0)
     weight_forward(KV)
-    collect(0)
     weight_forward(Q)
+    collect(1)
+    weight_start(OUT)
     share(0)
     weight_wait(KV)
     project(KV, 0)
     rs_step(KV, 1)
     weight_wait(Q)
     project(Q, 0)
+    rs_step(KV, 2)
     rs_step(Q, 1)
-    collect(1)
     weight_forward(OUT)
-    rs_step(KV, 2)
+    share(1)
+    rs_step(KV, 3)
     rs_step(Q, 2)
-    rs_step(KV, 3)
-    share(1)
     weight_wait(OUT)
+    project(OUT, 1)
+    rs_step(KV, 4)
     rs_step(Q, 3)
-    rs_step(KV, 4)
-    project(OUT, 1)
     rs_step(OUT, 1)
-    rs_step(Q, 4)
-
     own_keys = pl.ds(BACK * SLAB, SLAB)
     kvwin[own_keys, :] = rs_total(KV)
 
@@ -317,6 +298,7 @@
 
     for i in range(1, BACK + 1):
         kv_copy(i).start()
+    rs_step(Q, 4)
     rs_step(OUT, 2)
 
     def scale_of(values):
@@ -328,7 +310,6 @@
     for r in range(2):
         q = q_raw[:, HD * r : HD * r + HD].astype(F32)
         qh[SLAB * r : SLAB * r + SLAB, :] = (q * scale_of(q) * qgain).astype(BF16)
-    rs_step(OUT, 3)
 
     for i in range(1, BACK + 1):
         kv_copy(i).wait_recv()
@@ -341,12 +322,11 @@
         kh[rows, :] = (k * scale_of(k) * kgain).astype(BF16)
 
     scores[...] = dot(qh[...], kh[...], 1, 1)
-    rs_step(OUT, 4)
+    rs_step(OUT, 3)
     chunk = 32
     first_key = WINDOW - SLAB * place_in_ring
 
-    @pl.loop(0, 2 * SLAB // chunk)
-    def _(n):
+    def softmax(n):
         rows = pl.ds(pl.multiple_of(n * chunk, chunk), chunk)
         t0 = lax.rem(n, SLAB // chunk) * chunk
         t = t0 + lax.broadcasted_iota(jnp.int32, (chunk, 1), 0)
@@ -356,6 +336,9 @@
         e = jnp.exp(s - jnp.max(s, axis=-1, keepdims=True))
         pb[rows, :] = (e * (1.0 / jnp.sum(e, axis=-1, keepdims=True))).astype(BF16)
 
+    pl.loop(0, SLAB // chunk)(softmax)
+    rs_step(OUT, 4)
+    pl.loop(SLAB // chunk, 2 * SLAB // chunk)(softmax)
     blended = dot(pb[...], kvwin[:, HD:], 1, 0).astype(BF16)
     for r in range(2):
         gath[ATT, z, :, HD * r : HD * r + HD] = blended[SLAB * r : SLAB * r + SLAB]
@@ -366,17 +349,15 @@
         datt[SLAB * r : SLAB * r + SLAB, :] = total[:, HD * r : HD * r + HD]
 
     scores[...] = dot(datt[...], kvwin[:, HD:], 1, 1)
-    ag_step(ATT, 2)
-
-    @pl.loop(0, 2 * SLAB // chunk)
-    def _(n):
+
+    def softmax_back(n):
         rows = pl.ds(pl.multiple_of(n * chunk, chunk), chunk)
         p = pb[rows, :].astype(F32)
         dp = scores[rows, :]
         delta = jnp.sum(p * dp, axis=-1, keepdims=True)
         ds[rows, :] = (p * (dp - delta)).astype(BF16)
 
-    ag_step(ATT, 3)
+    pl.loop(0, 2 * SLAB // chunk)(softmax_back)
 
     def norm_back(raw, gain, grad):
         r = scale_of(raw)
@@ -402,7 +383,7 @@
 
     for i in range(1, BACK + 1):
         dk_copy(i).start()
-    ag_step(ATT, 4)
+    ag_step(ATT, 2)
 
     dqh = dot(ds[...], kh[...], 1, 0)
     for r in range(2):
@@ -411,7 +392,9 @@
             q_raw[:, lanes].astype(F32), qgain, dqh[SLAB * r : SLAB * r + SLAB]
         ).astype(BF16)
     ag_step(DQ, 1)
-    ag_step(ATT, 5)
+    ag_step(ATT, 3)
+    ag_step(DQ, 2)
+    ag_step(ATT, 4)
 
     def rl_copy(u, side):
         return remote(
@@ -451,74 +434,68 @@
         ).astype(BF16)
         return total[0:OWN]
 
-    def os_copy(t, i):
-        return remote(
-            ypart.at[t, rows_at(i)], ysib.at[t, i], s_os.at[t, i], r_os.at[t, i], row, sibling
+    def os_copy(t, dy, cc):
+        return remote(
+            ypart.at[t, rows_at(ys[dy]), half_at(1 - cc)], ysib.at[t, dy],
+            s_os.at[t, dy], r_os.at[t, dy], row, sibling,
         )
 
     def oy_copy(t, dy):
         return remote(
-            ypart.at[t, rows_at(ys[dy])], yrecv.at[t, dy - 1],
+            ypart.at[t, rows_at(ys[dy]), half_at(core)], yrecv.at[t, dy - 1],
             s_oy.at[t, dy], r_oy.at[t, dy], row, 2 * ys[dy] + core,
         )
 
-    def oz_copy(t, zt):
-        return remote(
-            ypart.at[t, rows_at(y), lanes_at(zt)], last.at[t, rows_at(quarter)],
-            s_oz.at[t, zt], r_oz.at[t, quarter], x * NZ + zt, col,
+    def oz_copy(t, j):
+        return remote(
+            ypart.at[t, rows_at(y), lanes_at(4 * core + j)], last.at[t, rows_at(quarter)],
+            s_oz.at[t, j], r_oz.at[t, quarter], x * NZ + 4 * core + j, 2 * y + head,
         )
 
     def oz_recv(t, j):
         slot = last.at[t, pl.ds(PITCH * j, SENT)]
-        return remote(slot, slot, s_oz.at[t, 0], r_oz.at[t, j], x * NZ + 4 * core + j, col)
+        return remote(
+            slot, slot, s_oz.at[t, j], r_oz.at[t, j], x * NZ + 4 * core + j, 2 * y + head
+        )
 
     def out_start(t):
-        @pl.when(jnp.logical_not(collects))
-        def _():
-            for i in range(NX):
-                os_copy(t, i).start()
+        for dy in (2, 1, 3, 0):
+            os_copy(t, dy, core).start()
 
     def out_middle(t):
-        @pl.when(collects)
-        def _():
-            for dy in (2, 1, 3, 0):
-                os_copy(t, ys[dy]).wait_recv()
-                rows = rows_at(ys[dy])
-                ypart[t, rows, :] = (
-                    ypart[t, rows, :].astype(F32) + ysib[t, ys[dy]].astype(F32)
-                ).astype(BF16)
-                if dy:
-                    oy_copy(t, dy).start()
+        for dy in (2, 1, 3, 0):
+            os_copy(t, dy, core).wait_recv()
+            rows, lanes = rows_at(ys[dy]), half_at(core)
+            ypart[t, rows, lanes] = (
+                ypart[t, rows, lanes].astype(F32) + ysib[t, dy].astype(F32)
+            ).astype(BF16)
+            if dy:
+                oy_copy(t, dy).start()
 
     def out_sum(t):
-        @pl.when(collects)
-        def _():
-            for dy in (1, 3, 2):
-                oy_copy(t, dy).wait_recv()
-            rows = rows_at(y)
-            total = ypart[t, rows, :].astype(F32)
-            for dy in (1, 2, 3):
-                total = total + yrecv[t, dy - 1].astype(F32)
-            ypart[t, rows, :] = total.astype(BF16)
-            for d in (4, 3, 5, 2, 6, 1, 7):
-                oz_copy(t, zs[d]).start()
-            last[t, rows_at(quarter), :] = ypart[t, rows, lanes_at(z)]
+        for dy in (1, 3, 2):
+            oy_copy(t, dy).wait_recv()
+        rows, lanes = rows_at(y), half_at(core)
+        total = ypart[t, rows, lanes].astype(F32)
+        for dy in (1, 2, 3):
+            total = total + yrecv[t, dy - 1].astype(F32)
+        ypart[t, rows, lanes] = total.astype(BF16)
+        for j in range(4):
+            @pl.when(4 * core + j != z)
+            def _():
+                oz_copy(t, j).start()
+
+            @pl.when(4 * core + j == z)
+            def _():
+                last[t, PITCH * j : PITCH * j + SENT] = ypart[t, rows, lanes_at(z)]
 
     def out_last(t, out):
         for j in range(4):
             @pl.when(4 * core + j != z)
             def _():
                 oz_recv(t, j).wait_recv()
-        out[...] = dot(last[t], place[...], 0, 1).astype(BF16)
-
-    grad_start(OUT, 1, ATT)
-    ag_step(DQ, 2)
-    ypart[0] = (
-        dot(w[OUT, :, 0:256], gathered(ATT, 0), 1, 1)
-        + dot(w[OUT, :, 256:512], gathered(ATT, 1), 1, 1)
-    ).astype(BF16)
-    out_start(0)
-    ag_step(DQ, 3)
+        for j in range(4):
+            out[OWN * j : OWN * j + OWN] = last[t, PITCH * j : PITCH * j + OWN]
 
     for i in range(1, BACK + 1):
         dk_copy(i).wait_recv()
@@ -527,34 +504,41 @@
         total = total + dkv_in[i].astype(F32)
     gath[DKV, z] = total.astype(BF16)
     ag_step(DKV, 1)
-
+    ag_step(DQ, 3)
+    ag_step(ATT, 5)
+    grad_start(OUT, 1, ATT)
+    ag_step(DKV, 2)
+    ag_step(DQ, 4)
+    ypart[0] = (
+        dot(w[OUT, :, 0:256], gathered(ATT, 0), 1, 1)
+        + dot(w[OUT, :, 256:512], gathered(ATT, 1), 1, 1)
+    ).astype(BF16)
+    out_start(0)
+    ag_step(DKV, 3)
     grad_middle(OUT)
-    ag_step(DQ, 4)
-    ag_step(DKV, 2)
+    ag_step(DQ, 5)
     out_middle(0)
-    ag_step(DQ, 5)
+    ag_step(DKV, 4)
     grad_start(Q, 0, DQ)
-    ag_step(DKV, 3)
-    ag_step(DKV, 4)
-    out_sum(0)
-    grad_middle(Q)
-    ag_step(DKV, 5)
-    grad_start(KV, 0, DKV)
-    total = (
+    rest[...] = (
         dot(w[Q, :, 0:256], gathered(DQ, 0), 1, 1) + dot(w[Q, :, 256:512], gathered(DQ, 1), 1, 1)
     )
+    ag_step(DKV, 5)
     ypart[1] = (
-        total
+        rest[...]
         + dot(w[KV, :, 0:256], gathered(DKV, 0), 1, 1)
         + dot(w[KV, :, 256:512], gathered(DKV, 1), 1, 1)
     ).astype(BF16)
     out_start(1)
+    grad_start(KV, 0, DKV)
+    out_middle(1)
+    grad_middle(Q)
     grad_middle(KV)
-    out_middle(1)
+    out_sum(0)
     go_out[...] = grad_last(OUT)
+    gq_out[...] = grad_last(Q)
+    out_sum(1)
     out_last(0, layer_out)
-    out_sum(1)
-    gq_out[...] = grad_last(Q)
     done = grad_last(KV)
     for h in (0, 1):
         gk_out[:, 128 * h : 128 * h + 128] = done[:, 256 * h : 256 * h + 128]
@@ -574,26 +558,23 @@
         for j in range(4):
             @pl.when(4 * core + j != z)
             def _():
-                piece_copy(t, j, 4 * core + j).wait_send()
-
-        @pl.when(collects)
-        def _():
-            for dy in (1, 2, 3):
+                piece_copy(t, j).wait_send()
+                oz_copy(t, j).wait_send()
+        for dy in range(NY):
+            share_copy(t, dy, core).wait_send()
+            os_copy(t, dy, core).wait_send()
+            if dy:
                 slab_copy(t, dy, y).wait_send()
                 oy_copy(t, dy).wait_send()
-            for dy in range(NY):
-                share_copy(t, dy).wait_send()
-            for d in range(1, NZ):
-                oz_copy(t, zs[d]).wait_send()
-
-        @pl.when(jnp.logical_not(collects))
-        def _():
-            for i in range(NX):
-                os_copy(t, i).wait_send()
 
     for i in range(1, BACK + 1):
         kv_copy(i).wait_send()
         dk_copy(i).wait_send()
+
+
+def hand_over(*refs):
+    for source, target in zip(refs[:6], refs[6:]):
+        target[...] = source[...]
 
 
 def shards(tokens, w_query, w_key, w_value, w_output, query_gain, key_gain, cotangent):
@@ -601,7 +582,7 @@
     dma = lambda *shape: pltpu.SemaphoreType.DMA(shape)
     spec = pl.BlockSpec(memory_space=pltpu.VMEM)
     scratch = [
-        vmem(4 * OWN, BLOCK), vmem(2, BLOCK, TOK), vmem(2, BLOCK, SUPER),
+        vmem(2, BLOCK, TOK), vmem(2, BLOCK, SUPER),
         vmem(3, BLOCK, 512), vmem(3, BLOCK, 512),
         vmem(3, NZ, SLAB, SLAB), vmem(3, 2, TOK, SLAB), vmem(3, 2, 3, SLAB, SLAB),
         vmem(3, NZ, SLAB, SLAB),
@@ -609,24 +590,25 @@
         vmem(2 * SLAB, KEYS, dtype=F32), vmem(2 * SLAB, KEYS), vmem(2 * SLAB, KEYS),
         vmem(2 * SLAB, HD),
         vmem(BACK, SLAB, 256), vmem(SLAB, 256, dtype=F32), vmem(BACK, SLAB, 256),
-        vmem(2, BLOCK, SUPER), vmem(2, NX, SENT, SUPER), vmem(2, 3, SENT, SUPER),
+        vmem(2, BLOCK, SUPER), vmem(BLOCK, SUPER, dtype=F32),
+        vmem(2, NY, SENT, 512), vmem(2, 3, SENT, 512),
         vmem(2, BLOCK, TOK), vmem(3, 2, SENT, 256), vmem(3, 2, SENT, 512),
         dma(3, 2), dma(3, 2), dma(3, 2), dma(3, 2),
-        dma(2, 4), dma(2, NZ), dma(2, NY), dma(2, NY), dma(2, NY), dma(2, NY), dma(2),
-        dma(3, 2, 4), dma(3, 2, 4), dma(3, 2, 4), dma(3, 2, 4), dma(1), dma(1),
+        dma(2, 4), dma(2, 4), dma(2, NY), dma(2, NY), dma(2, NY), dma(2, NY),
+        dma(3, 2, 4), dma(3, 2, 4), dma(3, 2, 4), dma(3, 2, 4),
         dma(BACK), dma(BACK), dma(BACK), dma(BACK),
         dma(3, 2), dma(3, 2), dma(3, 2), dma(3, 2),
-        dma(2, NX), dma(2, NX), dma(2, NY), dma(2, NY), dma(2, NZ), dma(2, 4),
+        dma(2, NY), dma(2, NY), dma(2, NY), dma(2, NY), dma(2, 4), dma(2, 4),
     ]
     outs = [
-        jax.ShapeDtypeStruct(tokens.shape, BF16),
-        jax.ShapeDtypeStruct(tokens.shape, BF16),
+        jax.ShapeDtypeStruct(tokens.shape[::-1], BF16),
+        jax.ShapeDtypeStruct(tokens.shape[::-1], BF16),
         jax.ShapeDtypeStruct(w_query.shape, BF16),
         jax.ShapeDtypeStruct(w_key.shape, BF16),
         jax.ShapeDtypeStruct(w_value.shape, BF16),
         jax.ShapeDtypeStruct(w_output.shape[::-1], BF16),
     ]
-    layer_out, input_grad, gq, gk, gv, go = pl.pallas_call(
+    results = pl.pallas_call(
         kernel,
         out_shape=outs,
         in_specs=[spec] * 8,
@@ -636,10 +618,13 @@
             collective_id=0, has_side_effects=True, vmem_limit_bytes=60 * 1024 * 1024
         ),
     )(
-        tokens, cotangent, w_query, w_key, w_value, w_output.T,
+        tokens.T, cotangent.T, w_query, w_key, w_value, w_output.T,
         query_gain.reshape(1, HD), key_gain.reshape(1, HD),
     )
-    return layer_out, input_grad, gq, gk, gv, go.T
+    layer_out, input_grad, gq, gk, gv, go = pl.pallas_call(
+        hand_over, out_shape=outs, in_specs=[spec] * 6, out_specs=[spec] * 6
+    )(*results)
+    return layer_out.T, input_grad.T, gq, gk, gv, go.T
 
 
 def solution(mesh):

time: 173 us -> 153 us (0.88); the launches traced: 171 us -> 153 us
  Pallas kernels: 163 us -> 152 us
  local copies, waits for them, and re-layouts: 8.18 us -> 0 us
    pallas_call x1, Pallas kernels: 163 us -> 150 us  [shards(): pl.pallas_call(kernel, out_shape=outs, in_specs=[spec] * 8, out_specs=[sp...]
    unnamed x20 -> x0, local copies, waits for them, and re-layouts: 8.18 us -> none
    pallas_call x0 -> x1, Pallas kernels: none -> 2.16 us  [shards(): pl.pallas_call(hand_over, out_shape=outs, in_specs=[spec] * 6, out_specs=...]
where the time goes in v3:
time: 153 us
  Pallas kernels  152 us (99%)
    pallas_call x1, Pallas kernels, shards(): pl.pallas_call(kernel, out_shape=outs, in_specs=[spec] * 8, out_specs=[sp...  150 us

profile of v3, /device:TPU:1, one launch (start us, length us, event | category | flops | bytes accessed | tf_op | source)
XLA Modules:
  0.0 153.1 jit_solution(14085736302575511563)
XLA Ops:
  0.6 150.3 %shard_map.127 = (bf16[672,128]{1,0:T(8,128)(2,1)}, bf16[672,128]{1,0:T(8,128)(2,1)}, bf16[168,512]{1,0:T(8,128)(2,1)}, bf16[168,256]{1,0:T(8,128)(2,1)}, bf16[1...) custom-call(bf16[672,128]{1,0:T(8,128)(2,1)} %bitcast.8, bf16[672,128]{1,0:T(8,128)(2,1)} %bitcast.9, ...), custom_call_target="tpu_custom_call" | custom-call | tf_op jit(solution)/shard_map/pallas_call | solution.py:611
  151.0 2.2 %shard_map.128 = (bf16[672,128]{1,0:T(8,128)(2,1)}, bf16[672,128]{1,0:T(8,128)(2,1)}, bf16[168,512]{1,0:T(8,128)(2,1)}, bf16[168,256]{1,0:T(8,128)(2,1)}, bf16[1...) custom-call(bf16[672,128]{1,0:T(8,128)(2,1)} %get-tuple-element.18.refs_0_, bf16[672,128]{1,0:T(8,128)(2,1)} %get-tuple-element.19.refs_1_, ...), custom_call_target="tpu_custom_call" | custom-call | tf_op jit(solution)/shard_map/pallas_call | solution.py:624

commit v4 on v3

--- a/solution.py
+++ b/solution.py
@@ -35,7 +35,7 @@
 def kernel(
     tok_in, cot_in, wq_in, wk_in, wv_in, wo_in, qg_ref, kg_ref,
     layer_out, input_grad, gq_out, gk_out, gv_out, go_out,
-    piece, slabs, w, g, part, sum_half, sum_full, gath,
+    piece, slabs, w, g, part, sums, gath,
     q_raw, qh, kh, kvwin, scores, pb, ds, datt, dkv, dkv_own, dkv_in,
     ypart, rest, ysib, yrecv, last, relay, full,
     s_xf, r_xf, s_xh, r_xh, s_p, r_p, s_y, r_y, s_s, r_s,
@@ -51,7 +51,10 @@
     zs = [ring(z + d, NZ) for d in range(NZ)]
     ys = [ring(y + d, NY) for d in range(NY)]
     sibling = col + 1 - 2 * core
-    place_in_ring = 4 * x + quarter
+    shift = 2 * core
+    ls = [ring(z + shift + d, NZ) for d in range(NZ)]
+    lz = ls[0]
+    place_in_ring = 4 * x + lax.rem(lz, 4)
 
     def remote(src, dst, ssem, rsem, to_row, to_col):
         return pltpu.make_async_remote_copy(
@@ -61,7 +64,7 @@
 
     def token_row(i):
         at = lax.rem(place_in_ring + 16 + i, 16)
-        return lax.div(at, 4) * NZ + 4 * head + lax.rem(at, 4)
+        return lax.div(at, 4) * NZ + ring(4 * lax.div(lz, 4) + lax.rem(at, 4) + NZ - shift, NZ)
 
     def x_row(side):
         return (xs[1] if side == 0 else xs[3]) * NZ + z
@@ -107,6 +110,11 @@
     w[Q, weight_rows, :] = wq_in[...]
     w[OUT, weight_rows, :] = wo_in[...]
 
+    for t, src in ((0, tok_in), (1, cot_in)):
+        for j in range(4):
+            piece[t, PITCH * j + 160 : PITCH * j + SENT] = jnp.zeros((SENT - 160, TOK), BF16)
+            piece[t, PITCH * j : PITCH * j + OWN] = src[OWN * j : OWN * j + OWN]
+
     pl.semaphore_wait(barrier, 20 - at_home.astype(jnp.int32))
 
     def xf_copy(u, side, xx):
@@ -148,7 +156,7 @@
     def piece_recv(t, j):
         slot = slabs.at[t, rows_at(y), lanes_at(4 * core + j)]
         return remote(
-            slot, slot, s_p.at[t, j], r_p.at[t, j], x * NZ + 4 * core + j, 2 * y + head
+            slot, slot, s_p.at[t, 0], r_p.at[t, j], x * NZ + 4 * core + j, 2 * y + head
         )
 
     def piece_start(t):
@@ -161,37 +169,37 @@
             def _():
                 slabs[t, rows_at(y), lanes_at(z)] = piece[t, PITCH * j : PITCH * j + SENT]
 
-    def slab_copy(t, dy, yy):
-        slot = slabs.at[t, rows_at(yy), half_at(core)]
-        return remote(slot, slot, s_y.at[t, dy], r_y.at[t, dy], row, 2 * ys[dy] + core)
+    def slab_copy(t, dy, j, yy):
+        slot = slabs.at[t, rows_at(yy), lanes_at(4 * core + j)]
+        return remote(slot, slot, s_y.at[t, dy, j], r_y.at[t, dy, j], row, 2 * ys[dy] + core)
 
     def share_copy(t, dy, cc):
         slot = slabs.at[t, rows_at(ys[(NY - dy) % NY]), half_at(cc)]
         return remote(slot, slot, s_s.at[t, dy], r_s.at[t, dy], row, sibling)
 
     def collect(t):
-        for j in range(4):
+        for i in range(4):
+            j = lax.rem(quarter + i, 4)
+
             @pl.when(4 * core + j != z)
             def _():
                 piece_recv(t, j).wait_recv()
-        for dy in (2, 1, 3):
-            slab_copy(t, dy, y).start()
+
+            for dy in (2, 1, 3):
+                slab_copy(t, dy, j, y).start()
         share_copy(t, 0, core).start()
 
     def share(t):
         for dy in (1, 3, 2):
-            slab_copy(t, dy, ys[NY - dy]).wait_recv()
+            for j in range(4):
+                slab_copy(t, dy, j, ys[NY - dy]).wait_recv()
             share_copy(t, dy, core).start()
         for dy in (0, 1, 3, 2):
             share_copy(t, dy, 1 - core).wait_recv()
 
-    for t, src in ((0, tok_in), (1, cot_in)):
-        for j in range(4):
-            piece[t, PITCH * j + 160 : PITCH * j + SENT] = jnp.zeros((SENT - 160, TOK), BF16)
-            piece[t, PITCH * j : PITCH * j + OWN] = src[OWN * j : OWN * j + OWN]
-        piece_start(t)
-        if t == 0:
-            weight_start(Q)
+    piece_start(0)
+    weight_start(Q)
+    piece_start(1)
     for j in range(4):
         gap = slice(PITCH * j + SENT, PITCH * (j + 1))
         for u in (KV, Q, OUT):
@@ -199,63 +207,71 @@
         for t in (0, 1):
             slabs[t, gap, :] = jnp.zeros((PITCH - SENT, SUPER), BF16)
 
-    def rs_copy(u, step, side):
-        if step == 1:
-            rows = pl.ds(TOK * side, TOK)
-            src, dst = part.at[u, zs[4], rows], sum_half.at[u, side]
-        else:
-            to = zs[5 - step] if side == 0 else zs[3 + step]
-            src, dst = part.at[u, to], sum_full.at[u, side, step - 2]
-        return remote(
-            src, dst, s_rs.at[u, side, step - 1], r_rs.at[u, side, step - 1], z_row(side), col
-        )
-
-    def rs_step(u, step):
-        for side in (0, 1):
-            if step > 1:
-                rs_copy(u, step - 1, side).wait_recv()
-                to = zs[5 - step] if side == 0 else zs[3 + step]
-                if step == 2:
-                    rows = slice(TOK * side, TOK * side + TOK)
-                    part[u, to, rows] = (
-                        part[u, to, rows].astype(F32) + sum_half[u, side].astype(F32)
-                    ).astype(BF16)
-                else:
-                    part[u, to] = (
-                        part[u, to].astype(F32) + sum_full[u, side, step - 3].astype(F32)
-                    ).astype(BF16)
-            rs_copy(u, step, side).start()
-
-    def rs_total(u):
-        rs_copy(u, 4, 0).wait_recv()
-        rs_copy(u, 4, 1).wait_recv()
+    def lane_half(sub):
+        return slice(HD * sub, HD * sub + HD)
+
+    def rs_copy(u, sub, step, side):
+        to = ls[5 - step] if side == 0 else ls[3 + step]
+        return remote(
+            part.at[u, to, :, pl.ds(HD * sub, HD)],
+            sums.at[u, side, step - 1, :, pl.ds(HD * sub, HD)],
+            s_rs.at[u, side, step - 1, sub], r_rs.at[u, side, step - 1, sub], z_row(side), col,
+        )
+
+    def rs_step(u, sub, n):
+        lanes = lane_half(sub)
+        for side in (sub, 1 - sub):
+            step = n if side == sub else n + 1
+            if step > 4:
+                continue
+            if n > 1:
+                rs_copy(u, sub, step - 1, side).wait_recv()
+                to = ls[5 - step] if side == 0 else ls[3 + step]
+                part[u, to, :, lanes] = (
+                    part[u, to, :, lanes].astype(F32) + sums[u, side, step - 2, :, lanes].astype(F32)
+                ).astype(BF16)
+            rs_copy(u, sub, step, side).start()
+
+    def rs_both(u, n):
+        rs_step(u, 0, n)
+        rs_step(u, 1, n)
+
+    def rs_total(u, sub):
+        lanes = lane_half(sub)
+        rs_copy(u, sub, 4, 1 - sub).wait_recv()
+        rs_copy(u, sub, 4, sub).wait_recv()
         return (
-            part[u, z].astype(F32)
-            + sum_full[u, 0, 2].astype(F32)
-            + sum_full[u, 1, 2].astype(F32)
+            part[u, lz, :, lanes].astype(F32)
+            + sums[u, 0, 3, :, lanes].astype(F32)
+            + sums[u, 1, 3, :, lanes].astype(F32)
         ).astype(BF16)
 
-    def ag_copy(v, step, side, sending):
+    def ag_copy(v, sub, step, side, sending):
         back = step - 1 if sending else step
-        slot = zs[(NZ - back) % NZ] if side == 0 else zs[back]
-        if step == 4:
-            rows = pl.ds(TOK * side, TOK)
-            block = gath.at[v, slot, rows]
-        else:
-            block = gath.at[v, slot]
-        return remote(
-            block, block, s_ag.at[v, side, step - 1], r_ag.at[v, side, step - 1], z_row(side), col
-        )
-
-    def ag_step(v, step):
-        for side in (0, 1):
-            if step > 1:
-                ag_copy(v, step - 1, side, False).wait_recv()
-            if step < 5:
-                ag_copy(v, step, side, True).start()
+        slot = ls[(NZ - back) % NZ] if side == 0 else ls[back]
+        block = gath.at[v, slot, :, pl.ds(HD * sub, HD)]
+        return remote(
+            block, block, s_ag.at[v, side, step - 1, sub], r_ag.at[v, side, step - 1, sub],
+            z_row(side), col,
+        )
+
+    def ag_step(v, sub, n):
+        for side in (sub, 1 - sub):
+            steps = 4 if side == sub else 3
+            if 1 <= n - 1 <= steps:
+                ag_copy(v, sub, n - 1, side, False).wait_recv()
+            if n <= steps:
+                ag_copy(v, sub, n, side, True).start()
+
+    def ag_both(v, n):
+        ag_step(v, 0, n)
+        ag_step(v, 1, n)
 
     def gathered(v, h):
         return gath[v, 4 * h : 4 * h + 4].reshape(SUPER, SLAB)
+
+    def gathered_half(v, h, sub):
+        return gath[v, 4 * h : 4 * h + 4, :, lane_half(sub)].reshape(SUPER, HD)
 
     def project(u, t):
         for h in (0, 1):
@@ -273,56 +289,63 @@
     share(0)
     weight_wait(KV)
     project(KV, 0)
-    rs_step(KV, 1)
+    rs_both(KV, 1)
     weight_wait(Q)
     project(Q, 0)
-    rs_step(KV, 2)
-    rs_step(Q, 1)
+    rs_both(KV, 2)
+    rs_both(Q, 1)
     weight_forward(OUT)
     share(1)
-    rs_step(KV, 3)
-    rs_step(Q, 2)
+    rs_both(KV, 3)
+    rs_both(Q, 2)
     weight_wait(OUT)
     project(OUT, 1)
-    rs_step(KV, 4)
-    rs_step(Q, 3)
-    rs_step(OUT, 1)
+    rs_both(KV, 4)
+    rs_both(Q, 3)
     own_keys = pl.ds(BACK * SLAB, SLAB)
-    kvwin[own_keys, :] = rs_total(KV)
-
-    def kv_copy(i):
-        return remote(
-            kvwin.at[own_keys], kvwin.at[pl.ds((BACK - i) * SLAB, SLAB)],
-            s_kv.at[i - 1], r_kv.at[i - 1], token_row(i), col,
-        )
-
-    for i in range(1, BACK + 1):
-        kv_copy(i).start()
-    rs_step(Q, 4)
-    rs_step(OUT, 2)
+
+    def kv_copy(i, sub):
+        lanes = pl.ds(HD * sub, HD)
+        return remote(
+            kvwin.at[own_keys, lanes], kvwin.at[pl.ds((BACK - i) * SLAB, SLAB), lanes],
+            s_kv.at[i - 1, sub], r_kv.at[i - 1, sub], token_row(i), col,
+        )
+
+    for sub in (0, 1):
+        kvwin[own_keys, lane_half(sub)] = rs_total(KV, sub)
+        for i in (3, 2, 1, 4):
+            kv_copy(i, sub).start()
+    rs_both(Q, 4)
+    rs_both(OUT, 1)
 
     def scale_of(values):
         return lax.rsqrt(jnp.mean(values * values, axis=-1, keepdims=True) + epsilon)
 
     qgain = qg_ref[...] * query_scalar ** (-0.5)
     kgain = kg_ref[...]
-    q_raw[...] = rs_total(Q)
-    for r in range(2):
-        q = q_raw[:, HD * r : HD * r + HD].astype(F32)
-        qh[SLAB * r : SLAB * r + SLAB, :] = (q * scale_of(q) * qgain).astype(BF16)
-
-    for i in range(1, BACK + 1):
-        kv_copy(i).wait_recv()
-
-
-    @pl.loop(0, BACK + 1)
-    def _(s):
-        rows = pl.ds(pl.multiple_of(s * SLAB, SLAB), SLAB)
+
+    def key_block(s):
+        rows = slice(s * SLAB, s * SLAB + SLAB)
         k = kvwin[rows, 0:HD].astype(F32)
         kh[rows, :] = (k * scale_of(k) * kgain).astype(BF16)
 
-    scores[...] = dot(qh[...], kh[...], 1, 1)
-    rs_step(OUT, 3)
+    key_block(BACK)
+    for r in range(2):
+        q_raw[:, lane_half(r)] = rs_total(Q, r)
+        q = q_raw[:, lane_half(r)].astype(F32)
+        qh[SLAB * r : SLAB * r + SLAB, :] = (q * scale_of(q) * qgain).astype(BF16)
+
+    def score_block(s):
+        rows = slice(s * SLAB, s * SLAB + SLAB)
+        scores[:, rows] = dot(qh[...], kh[rows, :], 1, 1)
+
+    score_block(BACK)
+    rs_both(OUT, 2)
+    for i in (1, 4, 2, 3):
+        kv_copy(i, 0).wait_recv()
+        key_block(BACK - i)
+        score_block(BACK - i)
+    rs_both(OUT, 3)
     chunk = 32
     first_key = WINDOW - SLAB * place_in_ring
 
@@ -337,17 +360,39 @@
         pb[rows, :] = (e * (1.0 / jnp.sum(e, axis=-1, keepdims=True))).astype(BF16)
 
     pl.loop(0, SLAB // chunk)(softmax)
-    rs_step(OUT, 4)
+    rs_both(OUT, 4)
     pl.loop(SLAB // chunk, 2 * SLAB // chunk)(softmax)
+    for i in range(1, BACK + 1):
+        kv_copy(i, 1).wait_recv()
+
+    def dk_copy(i, sub):
+        lanes = pl.ds(HD * sub, HD)
+        return remote(
+            dkv.at[BACK - i, :, lanes], dkv_in.at[i - 1, :, lanes],
+            s_dk.at[i - 1, sub], r_dk.at[i - 1, sub], token_row(-i), col,
+        )
+
+    def owned(sub):
+        for i in range(1, BACK + 1):
+            dk_copy(i, sub).wait_recv()
+        total = dkv_own[:, lane_half(sub)]
+        for i in range(BACK):
+            total = total + dkv_in[i, :, lane_half(sub)].astype(F32)
+        gath[DKV, lz, :, lane_half(sub)] = total.astype(BF16)
+
+    for r in range(2):
+        datt[SLAB * r : SLAB * r + SLAB, :] = rs_total(OUT, r)
+    dvh = dot(pb[...], datt[...], 0, 0)
+    dkv_own[:, HD:] = dvh[BACK * SLAB :]
+    for s in range(BACK):
+        dkv[s, :, HD:] = dvh[s * SLAB : s * SLAB + SLAB].astype(BF16)
+    for i in (3, 2, 1, 4):
+        dk_copy(i, 1).start()
+
     blended = dot(pb[...], kvwin[:, HD:], 1, 0).astype(BF16)
     for r in range(2):
-        gath[ATT, z, :, HD * r : HD * r + HD] = blended[SLAB * r : SLAB * r + SLAB]
-    ag_step(ATT, 1)
-
-    total = rs_total(OUT)
-    for r in range(2):
-        datt[SLAB * r : SLAB * r + SLAB, :] = total[:, HD * r : HD * r + HD]
-
+        gath[ATT, lz, :, lane_half(r)] = blended[SLAB * r : SLAB * r + SLAB]
+    ag_both(ATT, 1)
     scores[...] = dot(datt[...], kvwin[:, HD:], 1, 1)
 
     def softmax_back(n):
@@ -365,36 +410,27 @@
         return r * inner - raw * (r * r * r * jnp.mean(raw * inner, axis=-1, keepdims=True))
 
     dkh = dot(ds[...], qh[...], 0, 0)
-    dvh = dot(pb[...], datt[...], 0, 0)
     for s in range(BACK + 1):
         rows = slice(s * SLAB, s * SLAB + SLAB)
         dk = norm_back(kvwin[rows, 0:HD].astype(F32), kgain, dkh[rows])
         if s == BACK:
             dkv_own[:, 0:HD] = dk
-            dkv_own[:, HD:] = dvh[rows]
         else:
             dkv[s, :, 0:HD] = dk.astype(BF16)
-            dkv[s, :, HD:] = dvh[rows].astype(BF16)
-
-    def dk_copy(i):
-        return remote(
-            dkv.at[BACK - i], dkv_in.at[i - 1], s_dk.at[i - 1], r_dk.at[i - 1], token_row(-i), col
-        )
-
-    for i in range(1, BACK + 1):
-        dk_copy(i).start()
-    ag_step(ATT, 2)
+    for i in (3, 2, 1, 4):
+        dk_copy(i, 0).start()
+    ag_both(ATT, 2)
+    owned(1)
+    ag_step(DKV, 1, 1)
 
     dqh = dot(ds[...], kh[...], 1, 0)
     for r in range(2):
-        lanes = slice(HD * r, HD * r + HD)
-        gath[DQ, z, :, lanes] = norm_back(
-            q_raw[:, lanes].astype(F32), qgain, dqh[SLAB * r : SLAB * r + SLAB]
+        gath[DQ, lz, :, lane_half(r)] = norm_back(
+            q_raw[:, lane_half(r)].astype(F32), qgain, dqh[SLAB * r : SLAB * r + SLAB]
         ).astype(BF16)
-    ag_step(DQ, 1)
-    ag_step(ATT, 3)
-    ag_step(DQ, 2)
-    ag_step(ATT, 4)
+    ag_both(DQ, 1)
+    ag_both(ATT, 3)
+    ag_step(DKV, 1, 2)
 
     def rl_copy(u, side):
         return remote(
@@ -497,52 +533,57 @@
         for j in range(4):
             out[OWN * j : OWN * j + OWN] = last[t, PITCH * j : PITCH * j + OWN]
 
-    for i in range(1, BACK + 1):
-        dk_copy(i).wait_recv()
-    total = dkv_own[...]
-    for i in range(BACK):
-        total = total + dkv_in[i].astype(F32)
-    gath[DKV, z] = total.astype(BF16)
-    ag_step(DKV, 1)
-    ag_step(DQ, 3)
-    ag_step(ATT, 5)
+    owned(0)
+    ag_step(DKV, 0, 1)
+    ag_both(ATT, 4)
+    ag_both(DQ, 2)
+    ag_step(DKV, 0, 2)
+    ag_step(DKV, 1, 3)
+    ag_both(ATT, 5)
     grad_start(OUT, 1, ATT)
-    ag_step(DKV, 2)
-    ag_step(DQ, 4)
+    ag_step(DKV, 0, 3)
+    ag_both(DQ, 3)
+    ag_step(DKV, 1, 4)
     ypart[0] = (
         dot(w[OUT, :, 0:256], gathered(ATT, 0), 1, 1)
         + dot(w[OUT, :, 256:512], gathered(ATT, 1), 1, 1)
     ).astype(BF16)
     out_start(0)
-    ag_step(DKV, 3)
+    ag_step(DKV, 0, 4)
+    ag_both(DQ, 4)
     grad_middle(OUT)
-    ag_step(DQ, 5)
     out_middle(0)
-    ag_step(DKV, 4)
+    ag_step(DKV, 1, 5)
+    ag_both(DQ, 5)
+    rest[...] = (
+        dot(w[Q, :, 0:256], gathered(DQ, 0), 1, 1)
+        + dot(w[Q, :, 256:512], gathered(DQ, 1), 1, 1)
+        + dot(w[KV, :, 128:256], gathered_half(DKV, 0, 1), 1, 1)
+        + dot(w[KV, :, 384:512], gathered_half(DKV, 1, 1), 1, 1)
+    )
+    ag_step(DKV, 0, 5)
+    for dy in (2, 1, 3, 0):
+        rows = pl.ds(pl.multiple_of(PITCH * ys[dy], 16), PITCH)
+        ypart[1, rows, :] = (
+            rest[rows, :]
+            + dot(w[KV, rows, 0:128], gathered_half(DKV, 0, 0), 1, 1)
+            + dot(w[KV, rows, 256:384], gathered_half(DKV, 1, 0), 1, 1)
+        ).astype(BF16)
+        os_copy(1, dy, core).start()
+    out_middle(1)
     grad_start(Q, 0, DQ)
-    rest[...] = (
-        dot(w[Q, :, 0:256], gathered(DQ, 0), 1, 1) + dot(w[Q, :, 256:512], gathered(DQ, 1), 1, 1)
-    )
-    ag_step(DKV, 5)
-    ypart[1] = (
-        rest[...]
-        + dot(w[KV, :, 0:256], gathered(DKV, 0), 1, 1)
-        + dot(w[KV, :, 256:512], gathered(DKV, 1), 1, 1)
-    ).astype(BF16)
-    out_start(1)
     grad_start(KV, 0, DKV)
-    out_middle(1)
     grad_middle(Q)
     grad_middle(KV)
     out_sum(0)
     go_out[...] = grad_last(OUT)
+    out_sum(1)
     gq_out[...] = grad_last(Q)
-    out_sum(1)
-    out_last(0, layer_out)
     done = grad_last(KV)
     for h in (0, 1):
         gk_out[:, 128 * h : 128 * h + 128] = done[:, 256 * h : 256 * h + 128]
         gv_out[:, 128 * h : 128 * h + 128] = done[:, 256 * h + 128 : 256 * h + 256]
+    out_last(0, layer_out)
     out_last(1, input_grad)
 
     for u in (KV, Q, OUT):
@@ -551,9 +592,12 @@
             xh_copy(u, side, xs[3] if side == 0 else xs[1]).wait_send()
             rl_copy(u, side).wait_send()
             fl_copy(u, side).wait_send()
-            for step in range(1, 5):
-                rs_copy(u, step, side).wait_send()
-                ag_copy(u, step, side, True).wait_send()
+            for sub in (0, 1):
+                for step in range(1, 5):
+                    if step > 1 or side == sub:
+                        rs_copy(u, sub, step, side).wait_send()
+                    if step < 4 or side == sub:
+                        ag_copy(u, sub, step, side, True).wait_send()
     for t in (0, 1):
         for j in range(4):
             @pl.when(4 * core + j != z)
@@ -564,12 +608,14 @@
             share_copy(t, dy, core).wait_send()
             os_copy(t, dy, core).wait_send()
             if dy:
-                slab_copy(t, dy, y).wait_send()
+                for j in range(4):
+                    slab_copy(t, dy, j, y).wait_send()
                 oy_copy(t, dy).wait_send()
 
     for i in range(1, BACK + 1):
-        kv_copy(i).wait_send()
-        dk_copy(i).wait_send()
+        for sub in (0, 1):
+            kv_copy(i, sub).wait_send()
+            dk_copy(i, sub).wait_send()
 
 
 def hand_over(*refs):
@@ -584,7 +630,7 @@
     scratch = [
         vmem(2, BLOCK, TOK), vmem(2, BLOCK, SUPER),
         vmem(3, BLOCK, 512), vmem(3, BLOCK, 512),
-        vmem(3, NZ, SLAB, SLAB), vmem(3, 2, TOK, SLAB), vmem(3, 2, 3, SLAB, SLAB),
+        vmem(3, NZ, SLAB, SLAB), vmem(3, 2, 4, SLAB, SLAB),
         vmem(3, NZ, SLAB, SLAB),
         vmem(SLAB, SLAB), vmem(2 * SLAB, HD), vmem(KEYS, HD), vmem(KEYS, 2 * HD),
         vmem(2 * SLAB, KEYS, dtype=F32), vmem(2 * SLAB, KEYS), vmem(2 * SLAB, KEYS),
@@ -594,9 +640,9 @@
         vmem(2, NY, SENT, 512), vmem(2, 3, SENT, 512),
         vmem(2, BLOCK, TOK), vmem(3, 2, SENT, 256), vmem(3, 2, SENT, 512),
         dma(3, 2), dma(3, 2), dma(3, 2), dma(3, 2),
-        dma(2, 4), dma(2, 4), dma(2, NY), dma(2, NY), dma(2, NY), dma(2, NY),
-        dma(3, 2, 4), dma(3, 2, 4), dma(3, 2, 4), dma(3, 2, 4),
-        dma(BACK), dma(BACK), dma(BACK), dma(BACK),
+        dma(2, 4), dma(2, 4), dma(2, NY, 4), dma(2, NY, 4), dma(2, NY), dma(2, NY),
+        dma(3, 2, 4, 2), dma(3, 2, 4, 2), dma(3, 2, 4, 2), dma(3, 2, 4, 2),
+        dma(BACK, 2), dma(BACK, 2), dma(BACK, 2), dma(BACK, 2),
         dma(3, 2), dma(3, 2), dma(3, 2), dma(3, 2),
         dma(2, NY), dma(2, NY), dma(2, NY), dma(2, NY), dma(2, 4), dma(2, 4),
     ]

time: 153 us -> 147 us (0.961)
  Pallas kernels: 152 us -> 146 us
    pallas_call x1, Pallas kernels: 150 us -> 144 us  [shards(): pl.pallas_call(kernel, out_shape=outs, in_specs=[spec] * 8, out_specs=[sp...]
where the time goes in v4:
time: 147 us
  Pallas kernels  146 us (99%)
    pallas_call x1, Pallas kernels, shards(): pl.pallas_call(kernel, out_shape=outs, in_specs=[spec] * 8, out_specs=[sp...  144 us

profile of v4, /device:TPU:1, one launch (start us, length us, event | category | flops | bytes accessed | tf_op | source)
XLA Modules:
  0.0 146.7 jit_solution(18240532619586308226)
XLA Ops:
  0.6 143.9 %shard_map.127 = (bf16[672,128]{1,0:T(8,128)(2,1)}, bf16[672,128]{1,0:T(8,128)(2,1)}, bf16[168,512]{1,0:T(8,128)(2,1)}, bf16[168,256]{1,0:T(8,128)(2,1)}, bf16[1...) custom-call(bf16[672,128]{1,0:T(8,128)(2,1)} %bitcast.8, bf16[672,128]{1,0:T(8,128)(2,1)} %bitcast.9, ...), custom_call_target="tpu_custom_call" | custom-call | tf_op jit(solution)/shard_map/pallas_call | solution.py:657
  144.6 2.2 %shard_map.128 = (bf16[672,128]{1,0:T(8,128)(2,1)}, bf16[672,128]{1,0:T(8,128)(2,1)}, bf16[168,512]{1,0:T(8,128)(2,1)}, bf16[168,256]{1,0:T(8,128)(2,1)}, bf16[1...) custom-call(bf16[672,128]{1,0:T(8,128)(2,1)} %get-tuple-element.18.refs_0_, bf16[672,128]{1,0:T(8,128)(2,1)} %get-tuple-element.19.refs_1_, ...), custom_call_target="tpu_custom_call" | custom-call | tf_op jit(solution)/shard_map/pallas_call | solution.py:670

commit v5 on v4

--- a/solution.py
+++ b/solution.py
@@ -274,12 +274,9 @@
         return gath[v, 4 * h : 4 * h + 4, :, lane_half(sub)].reshape(SUPER, HD)
 
     def project(u, t):
+        product = dot(slabs[t], w[u], 0, 0).astype(BF16)
         for h in (0, 1):
-            part[u, 4 * h : 4 * h + 4] = (
-                dot(slabs[t], w[u, :, 256 * h : 256 * h + 256], 0, 0)
-                .astype(BF16)
-                .reshape(4, SLAB, SLAB)
-            )
+            part[u, 4 * h : 4 * h + 4] = product[:, 256 * h : 256 * h + 256].reshape(4, SLAB, SLAB)
 
     collect(0)
     weight_forward(KV)
@@ -302,6 +299,7 @@
     project(OUT, 1)
     rs_both(KV, 4)
     rs_both(Q, 3)
+    rs_both(OUT, 1)
     own_keys = pl.ds(BACK * SLAB, SLAB)
 
     def kv_copy(i, sub):
@@ -315,8 +313,8 @@
         kvwin[own_keys, lane_half(sub)] = rs_total(KV, sub)
         for i in (3, 2, 1, 4):
             kv_copy(i, sub).start()
-    rs_both(Q, 4)
-    rs_both(OUT, 1)
+        if sub == 0:
+            rs_both(Q, 4)
 
     def scale_of(values):
         return lax.rsqrt(jnp.mean(values * values, axis=-1, keepdims=True) + epsilon)
@@ -346,7 +344,7 @@
         key_block(BACK - i)
         score_block(BACK - i)
     rs_both(OUT, 3)
-    chunk = 32
+    chunk = 64
     first_key = WINDOW - SLAB * place_in_ring
 
     def softmax(n):
@@ -380,6 +378,10 @@
             total = total + dkv_in[i, :, lane_half(sub)].astype(F32)
         gath[DKV, lz, :, lane_half(sub)] = total.astype(BF16)
 
+    blended = dot(pb[...], kvwin[:, HD:], 1, 0).astype(BF16)
+    for r in range(2):
+        gath[ATT, lz, :, lane_half(r)] = blended[SLAB * r : SLAB * r + SLAB]
+    ag_both(ATT, 1)
     for r in range(2):
         datt[SLAB * r : SLAB * r + SLAB, :] = rs_total(OUT, r)
     dvh = dot(pb[...], datt[...], 0, 0)
@@ -389,10 +391,6 @@
     for i in (3, 2, 1, 4):
         dk_copy(i, 1).start()
 
-    blended = dot(pb[...], kvwin[:, HD:], 1, 0).astype(BF16)
-    for r in range(2):
-        gath[ATT, lz, :, lane_half(r)] = blended[SLAB * r : SLAB * r + SLAB]
-    ag_both(ATT, 1)
     scores[...] = dot(datt[...], kvwin[:, HD:], 1, 1)
 
     def softmax_back(n):
@@ -476,10 +474,11 @@
             s_os.at[t, dy], r_os.at[t, dy], row, sibling,
         )
 
-    def oy_copy(t, dy):
-        return remote(
-            ypart.at[t, rows_at(ys[dy]), half_at(core)], yrecv.at[t, dy - 1],
-            s_oy.at[t, dy], r_oy.at[t, dy], row, 2 * ys[dy] + core,
+    def oy_copy(t, dy, j):
+        return remote(
+            ypart.at[t, rows_at(ys[dy]), lanes_at(4 * core + j)],
+            yrecv.at[t, dy - 1, :, pl.ds(TOK * j, TOK)],
+            s_oy.at[t, dy, j], r_oy.at[t, dy, j], row, 2 * ys[dy] + core,
         )
 
     def oz_copy(t, j):
@@ -505,25 +504,31 @@
             ypart[t, rows, lanes] = (
                 ypart[t, rows, lanes].astype(F32) + ysib[t, dy].astype(F32)
             ).astype(BF16)
-            if dy:
-                oy_copy(t, dy).start()
+            if dy == 2:
+                for j in range(4):
+                    oy_copy(t, 2, j).start()
+            if dy == 3:
+                for j in range(4):
+                    oy_copy(t, 1, j).start()
+                    oy_copy(t, 3, j).start()
 
     def out_sum(t):
-        for dy in (1, 3, 2):
-            oy_copy(t, dy).wait_recv()
-        rows, lanes = rows_at(y), half_at(core)
-        total = ypart[t, rows, lanes].astype(F32)
-        for dy in (1, 2, 3):
-            total = total + yrecv[t, dy - 1].astype(F32)
-        ypart[t, rows, lanes] = total.astype(BF16)
+        rows = rows_at(y)
         for j in range(4):
+            lanes = lanes_at(4 * core + j)
+            total = ypart[t, rows, lanes].astype(F32)
+            for dy in (2, 1, 3):
+                oy_copy(t, dy, j).wait_recv()
+                total = total + yrecv[t, dy - 1, :, TOK * j : TOK * j + TOK].astype(F32)
+            ypart[t, rows, lanes] = total.astype(BF16)
+
             @pl.when(4 * core + j != z)
             def _():
                 oz_copy(t, j).start()
 
             @pl.when(4 * core + j == z)
             def _():
-                last[t, PITCH * j : PITCH * j + SENT] = ypart[t, rows, lanes_at(z)]
+                last[t, PITCH * j : PITCH * j + SENT] = total.astype(BF16)
 
     def out_last(t, out):
         for j in range(4):
@@ -561,6 +566,7 @@
         + dot(w[KV, :, 128:256], gathered_half(DKV, 0, 1), 1, 1)
         + dot(w[KV, :, 384:512], gathered_half(DKV, 1, 1), 1, 1)
     )
+    grad_start(Q, 0, DQ)
     ag_step(DKV, 0, 5)
     for dy in (2, 1, 3, 0):
         rows = pl.ds(pl.multiple_of(PITCH * ys[dy], 16), PITCH)
@@ -571,7 +577,6 @@
         ).astype(BF16)
         os_copy(1, dy, core).start()
     out_middle(1)
-    grad_start(Q, 0, DQ)
     grad_start(KV, 0, DKV)
     grad_middle(Q)
     grad_middle(KV)
@@ -610,7 +615,7 @@
             if dy:
                 for j in range(4):
                     slab_copy(t, dy, j, y).wait_send()
-                oy_copy(t, dy).wait_send()
+                    oy_copy(t, dy, j).wait_send()
 
     for i in range(1, BACK + 1):
         for sub in (0, 1):
@@ -644,7 +649,7 @@
         dma(3, 2, 4, 2), dma(3, 2, 4, 2), dma(3, 2, 4, 2), dma(3, 2, 4, 2),
         dma(BACK, 2), dma(BACK, 2), dma(BACK, 2), dma(BACK, 2),
         dma(3, 2), dma(3, 2), dma(3, 2), dma(3, 2),
-        dma(2, NY), dma(2, NY), dma(2, NY), dma(2, NY), dma(2, 4), dma(2, 4),
+        dma(2, NY), dma(2, NY), dma(2, NY, 4), dma(2, NY, 4), dma(2, 4), dma(2, 4),
     ]
     outs = [
         jax.ShapeDtypeStruct(tokens.shape[::-1], BF16),

time: 147 us -> 143 us (0.973)
  Pallas kernels: 146 us -> 142 us
    pallas_call x1, Pallas kernels: 144 us -> 140 us  [shards(): pl.pallas_call(kernel, out_shape=outs, in_specs=[spec] * 8, out_specs=[sp...]
where the time goes in v5:
time: 143 us
  Pallas kernels  142 us (99%)
    pallas_call x1, Pallas kernels, shards(): pl.pallas_call(kernel, out_shape=outs, in_specs=[spec] * 8, out_specs=[sp...  140 us

profile of v5, /device:TPU:1, one launch (start us, length us, event | category | flops | bytes accessed | tf_op | source)
XLA Modules:
  0.0 142.6 jit_solution(5281091862172413034)
XLA Ops:
  0.6 139.8 %shard_map.127 = (bf16[672,128]{1,0:T(8,128)(2,1)}, bf16[672,128]{1,0:T(8,128)(2,1)}, bf16[168,512]{1,0:T(8,128)(2,1)}, bf16[168,256]{1,0:T(8,128)(2,1)}, bf16[1...) custom-call(bf16[672,128]{1,0:T(8,128)(2,1)} %bitcast.8, bf16[672,128]{1,0:T(8,128)(2,1)} %bitcast.9, ...), custom_call_target="tpu_custom_call" | custom-call | tf_op jit(solution)/shard_map/pallas_call | solution.py:662
  140.4 2.2 %shard_map.128 = (bf16[672,128]{1,0:T(8,128)(2,1)}, bf16[672,128]{1,0:T(8,128)(2,1)}, bf16[168,512]{1,0:T(8,128)(2,1)}, bf16[168,256]{1,0:T(8,128)(2,1)}, bf16[1...) custom-call(bf16[672,128]{1,0:T(8,128)(2,1)} %get-tuple-element.18.refs_0_, bf16[672,128]{1,0:T(8,128)(2,1)} %get-tuple-element.19.refs_1_, ...), custom_call_target="tpu_custom_call" | custom-call | tf_op jit(solution)/shard_map/pallas_call | solution.py:675

commit v6 on v5

--- a/solution.py
+++ b/solution.py
@@ -139,8 +139,6 @@
         xh_copy(u, 0, xs[2]).wait_recv()
         xh_copy(u, 1, xs[2]).wait_recv()
 
-    weight_start(KV)
-
     def lanes_at(i):
         return pl.ds(pl.multiple_of(TOK * i, TOK), TOK)
 
@@ -185,7 +183,7 @@
             def _():
                 piece_recv(t, j).wait_recv()
 
-            for dy in (2, 1, 3):
+            for dy in (1, 3, 2):
                 slab_copy(t, dy, j, y).start()
         share_copy(t, 0, core).start()
 
@@ -198,6 +196,7 @@
             share_copy(t, dy, 1 - core).wait_recv()
 
     piece_start(0)
+    weight_start(KV)
     weight_start(Q)
     piece_start(1)
     for j in range(4):
@@ -281,9 +280,9 @@
     collect(0)
     weight_forward(KV)
     weight_forward(Q)
-    collect(1)
     weight_start(OUT)
     share(0)
+    collect(1)
     weight_wait(KV)
     project(KV, 0)
     rs_both(KV, 1)
@@ -400,7 +399,9 @@
         delta = jnp.sum(p * dp, axis=-1, keepdims=True)
         ds[rows, :] = (p * (dp - delta)).astype(BF16)
 
-    pl.loop(0, 2 * SLAB // chunk)(softmax_back)
+    pl.loop(0, SLAB // chunk)(softmax_back)
+    ag_both(ATT, 2)
+    pl.loop(SLAB // chunk, 2 * SLAB // chunk)(softmax_back)
 
     def norm_back(raw, gain, grad):
         r = scale_of(raw)
@@ -417,7 +418,6 @@
             dkv[s, :, 0:HD] = dk.astype(BF16)
     for i in (3, 2, 1, 4):
         dk_copy(i, 0).start()
-    ag_both(ATT, 2)
     owned(1)
     ag_step(DKV, 1, 1)
 

time: 143 us -> 140 us (0.979)
  Pallas kernels: 142 us -> 140 us
    pallas_call x1, Pallas kernels: 140 us -> 138 us  [shards(): pl.pallas_call(kernel, out_shape=outs, in_specs=[spec] * 8, out_specs=[sp...]
where the time goes in v6:
time: 140 us
  Pallas kernels  140 us (100%)
    pallas_call x1, Pallas kernels, shards(): pl.pallas_call(kernel, out_shape=outs, in_specs=[spec] * 8, out_specs=[sp...  138 us

profile of v6, /device:TPU:1, one launch (start us, length us, event | category | flops | bytes accessed | tf_op | source)
XLA Modules:
  0.0 140.3 jit_solution(304484379662127271)
XLA Ops:
  0.6 137.5 %shard_map.127 = (bf16[672,128]{1,0:T(8,128)(2,1)}, bf16[672,128]{1,0:T(8,128)(2,1)}, bf16[168,512]{1,0:T(8,128)(2,1)}, bf16[168,256]{1,0:T(8,128)(2,1)}, bf16[1...) custom-call(bf16[672,128]{1,0:T(8,128)(2,1)} %bitcast.8, bf16[672,128]{1,0:T(8,128)(2,1)} %bitcast.9, ...), custom_call_target="tpu_custom_call" | custom-call | tf_op jit(solution)/shard_map/pallas_call | solution.py:662
  138.2 2.2 %shard_map.128 = (bf16[672,128]{1,0:T(8,128)(2,1)}, bf16[672,128]{1,0:T(8,128)(2,1)}, bf16[168,512]{1,0:T(8,128)(2,1)}, bf16[168,256]{1,0:T(8,128)(2,1)}, bf16[1...) custom-call(bf16[672,128]{1,0:T(8,128)(2,1)} %get-tuple-element.18.refs_0_, bf16[672,128]{1,0:T(8,128)(2,1)} %get-tuple-element.19.refs_1_, ...), custom_call_target="tpu_custom_call" | custom-call | tf_op jit(solution)/shard_map/pallas_call | solution.py:675
